TPU v7x, 32 devices: a whole 2x2x4 slice. The times are simulated.
32 devices in a mesh: view: 4 (over y, x), row: 4 (over z), disp: 2 (over core).
Axes of the slice: x: 2, y: 2, z: 4, core: 2. Of those that a mesh axis runs over, the one named last changes fastest.
Arguments:
- images: float32 [4, 32, 2048], P('view', 'row')
- sharpness: float32 [4], P('view'), may hold values from 1 to 800
- paired: int32 [4, 2], P('view'), may hold values from 0 to 1, as said below
- offset: int32 [4, 2], P('view'), may hold values from 0 to 127
- row_range: int32 [4, 2, 2], P('view'), may hold values from 0 to 32, as said below
Outputs:
- left_disparity: float32 [4, 2, 32, 2048], P('view', None, 'row')
- right_disparity: float32 [4, 2, 32, 2048], P('view', None, 'row')
Inputs may be any that keep to these rules, and one draw needn't show every extreme that they name: paired[v, j] is 0 whenever v + j + 1 >= 4. row_range[v, j, 0] <= 8 and row_range[v, j, 1] >= 24.
All inputs are finite; a program needn't handle non-finite values.
Results may differ from a plain program's by a relative error of at most 0.0003.
Values sent between devices are 32-bit elements; how exact they have to be, the bound alone decides.
A program may use at most 192 MiB of HBM per device.

v0:
```python
import functools
import math

import jax
import jax.numpy as jnp
from jax import lax
from jax.experimental import pallas as pl
from jax.experimental.pallas import tpu as pltpu
from jax.sharding import PartitionSpec as P

DISP = 256
RAD = 4
TAPS = 2 * RAD + 1
EPSILON = 1e-05
DEPTH = 256
PAD = 128
FAR = -1e30


def rounded(value):
    return value.astype(jnp.bfloat16).astype(jnp.float32)


def split3(value):
    high = rounded(value)
    middle = rounded(value - high)
    return (high, middle, value - high - middle)


def build_patches(pad_ref, stat_ref, tail_ref, patch_ref, gain, valid, extras, order):
    cols = patch_ref.shape[1]
    top = pad_ref[0:8, :]
    last = pad_ref[8:9, :]
    stat_ref[0:1, :] = jnp.sum(top, axis=0, keepdims=True) + last
    stat_ref[1:2, :] = jnp.sum(top * top, axis=0, keepdims=True) + last * last
    total = stat_ref[0:2, PAD - RAD : PAD - RAD + cols]
    for tap in range(1, TAPS):
        begin = PAD - RAD + tap
        total = total + stat_ref[0:2, begin : begin + cols]
    total = total * (1.0 / (TAPS * TAPS))
    mean = total[0:1]
    var = total[1:2] - mean * mean
    scale = lax.rsqrt(var + EPSILON) * (gain * (1.0 / TAPS))
    if valid is not None:
        scale = jnp.where(valid, scale, 0.0)
    for tap in range(TAPS):
        begin = PAD - RAD + tap
        tail_ref[tap : tap + 1, :] = pad_ref[8:9, begin : begin + cols]
        value = (pad_ref[0:8, begin : begin + cols] - mean) * scale
        high = rounded(value)
        parts = (high, value - high)
        for group in range(3):
            start = group * 8 * TAPS + tap * 8
            patch_ref[start : start + 8, :] = parts[order[group]]
    value = (tail_ref[0:TAPS, :] - mean) * scale
    high = rounded(value)
    parts = (high, value - high)
    for group in range(3):
        start = 24 * TAPS + group * TAPS
        patch_ref[start : start + TAPS, :] = parts[order[group]]
    base = 27 * TAPS
    patch_ref[base:DEPTH, :] = jnp.zeros((DEPTH - base, cols), jnp.float32)
    for place, row in extras:
        patch_ref[base + place : base + place + 1, :] = row


def soft_block(score_ref, result_ref, start, left):
    lane = lax.broadcasted_iota(jnp.int32, (8, 128), 1)
    sub = lax.broadcasted_iota(jnp.int32, (8, 128), 0)
    skew = lane - sub
    sub_f = sub.astype(jnp.float32)
    lane_f = lane[0:1].astype(jnp.float32)
    slack = 0 if left else 1
    steps = DISP // 8
    corner = 128 // 8
    for half in range(2):

        def load(step):
            row = half * 128 + step * 8
            return score_ref[row : row + 8, half * 128 : half * 128 + 128]

        near = [skew < 8 * step + slack for step in range(corner)]
        scores = [jnp.where(near[step], load(step), load(step + steps)) for step in range(corner)]
        scores += [load(step) for step in range(corner, steps)]
        tops = scores[:4]
        for step in range(4, steps):
            tops[step % 4] = jnp.maximum(tops[step % 4], scores[step])
        top = jnp.maximum(jnp.maximum(tops[0], tops[1]), jnp.maximum(tops[2], tops[3]))
        top = jnp.broadcast_to(jnp.max(top, axis=0, keepdims=True), (8, 128))
        zero = jnp.zeros((8, 128), jnp.float32)
        summed, running, far = ([zero, zero], [zero, zero], [zero, zero])
        for step in range(steps):
            weight = jnp.exp2(scores[step] - top)
            if step < corner:
                far[step % 2] = far[step % 2] + jnp.where(near[step], 0.0, weight)
            summed[step % 2] = summed[step % 2] + weight
            running[step % 2] = running[step % 2] + summed[step % 2]
        both = summed[0] + summed[1]
        moment = 8.0 * (steps * both - 2.0 * (running[0] + running[1]) + summed[1])
        moment = moment + sub_f * both + float(DISP) * (far[0] + far[1])
        total = jnp.sum(both, axis=0, keepdims=True)
        moment = jnp.sum(moment, axis=0, keepdims=True)
        if left:
            weighted = (lane_f + DISP) * total - moment
        else:
            weighted = moment - lane_f * total
        column = pl.multiple_of(start + half * 128, 128)
        result_ref[:, pl.ds(column, 128)] = weighted / (total * DISP)


def soft_both(left_rows, left_cols, right_rows, right_cols, left_score, right_score, left_result, right_result):
    count = left_result.shape[1] // 256

    def scores(rows_ref, cols_ref, score_ref, start):
        score_ref[...] = jnp.dot(
            rows_ref[pl.ds(start, 512), :],
            cols_ref[:, pl.ds(start, 256)],
            preferred_element_type=jnp.float32,
        )

    unroll = math.gcd(count, 4)

    def body(step, carry):
        for inner in range(unroll):
            block = step * unroll + inner
            start = pl.multiple_of(block * 256, 256)
            after = pl.multiple_of(jnp.minimum(block + 1, count - 1) * 256, 256)
            scores(left_rows, right_cols, right_score, start)
            soft_block(left_score, left_result, start, True)
            scores(right_rows, left_cols, left_score, after)
            soft_block(right_score, right_result, start, False)
        return carry

    scores(right_rows, left_cols, left_score, 0)
    lax.fori_loop(0, count // unroll, body, 0)


def row_of(view, disp, row_count):
    group = lax.axis_size("view") * lax.axis_size("disp")
    return (view * lax.axis_size("disp") + disp) * row_count // group


def match_kernel(
    views, slots, row_count, meta_ref, bands_ref, out_ref,
    pad_ref, roll_ref, stat_ref, tail_ref, patch_ref,
    left_cols, left_rows, right_cols, right_rows, left_score, right_score, left_result, right_result,
):
    cols = patch_ref.shape[1]
    out_ref[...] = jnp.zeros_like(out_ref)
    pad_ref[...] = jnp.zeros_like(pad_ref)
    column = lax.broadcasted_iota(jnp.int32, (1, cols), 1)
    depth_at = lax.broadcasted_iota(jnp.int32, (1, DEPTH), 1) - 27 * TAPS
    ones = jnp.ones((1, cols), jnp.float32)
    flag = jnp.where((depth_at >= 0) & (depth_at < 6), 1.0, 0.0)
    local = row_of(lax.axis_index("view"), lax.axis_index("disp"), row_count)
    row = (lax.axis_index("row") * row_count + local).astype(jnp.float32)
    for view in range(views):
        moved = pltpu.roll(bands_ref[view], 2 * row_count + RAD - local, 0)
        pad_ref[view, 0:TAPS, PAD : PAD + cols] = moved[0:TAPS]
    for view in range(1, views):
        build_patches(
            pad_ref.at[view], stat_ref, tail_ref, patch_ref, 1.0, None,
            [(3, ones), (4, ones), (5, ones)], (0, 1, 0),
        )
        whole = patch_ref[...].astype(jnp.bfloat16)
        right_cols[view - 1] = whole
        right_rows[view - 1, 0:DISP, :] = jnp.broadcast_to(flag, (DISP, DEPTH)).astype(jnp.bfloat16)
        right_rows[view - 1, DISP : DISP + cols, :] = whole.T
    for view in range(views - 1):
        for slot in range(min(slots, views - 1 - view)):
            partner = view + slot + 1
            pairing = meta_ref[view, 0, 1 + slot]
            first_row = meta_ref[view, 0, 1 + 2 * slots + 2 * slot]
            end_row = meta_ref[view, 0, 2 + 2 * slots + 2 * slot]

            @pl.when((pairing != 0.0) & (row >= first_row) & (row < end_row))
            def _():
                shift = meta_ref[view, 0, 1 + slots + slot].astype(jnp.int32)
                keep = jnp.full((1, cols), pairing, jnp.float32)
                gain = meta_ref[view, 0, 0] * math.log2(math.e)
                roll_ref[...] = pltpu.roll(pad_ref[view], cols + 2 * PAD - shift, 1)
                valid = column < cols - shift
                floor = [-part for part in split3(jnp.full((1, cols), gain, jnp.float32))]
                extras = [(place, floor[place]) for place in range(3)]
                extras += [(place + 3, jnp.where(valid, 0.0, floor[place])) for place in range(3)]
                build_patches(
                    roll_ref, stat_ref, tail_ref, patch_ref, gain, valid, extras, (0, 0, 1)
                )
                whole = patch_ref[...].astype(jnp.bfloat16)
                left_cols[...] = whole
                left_rows[0:cols, :] = whole.T
                splits = [-part for part in split3(jnp.full((1, DEPTH), gain, jnp.float32))]
                ends = jnp.zeros((1, DEPTH), jnp.float32)
                for place in range(6):
                    ends = jnp.where(depth_at == place, splits[place % 3], ends)
                left_rows[cols : cols + DISP, :] = jnp.broadcast_to(ends, (DISP, DEPTH)).astype(jnp.bfloat16)
                soft_both(
                    left_rows, left_cols, right_rows.at[partner - 1], right_cols.at[partner - 1],
                    left_score, right_score, left_result, right_result,
                )
                moved = pltpu.roll(jnp.broadcast_to(left_result[...], (8, cols)), shift, 1)[0:1]
                even = (DISP - 1) / (2.0 * DISP)
                out_ref[view, slot : slot + 1, :] = jnp.where(column < shift, even, moved) * keep
                place = slots + slot
                out_ref[partner, place : place + 1, :] = right_result[...] * keep


def match(meta, bands, slots):
    views, rows, cols = bands.shape
    smem = pl.BlockSpec(memory_space=pltpu.SMEM)
    vmem = pl.BlockSpec(memory_space=pltpu.VMEM)
    wide = cols + 2 * PAD
    return pl.pallas_call(
        functools.partial(match_kernel, views, slots, rows // 3),
        out_shape=jax.ShapeDtypeStruct((views, 2 * slots, cols), jnp.float32),
        in_specs=[smem, vmem],
        out_specs=vmem,
        scratch_shapes=[
            pltpu.VMEM((views, 16, wide), jnp.float32),
            pltpu.VMEM((16, wide), jnp.float32),
            pltpu.VMEM((8, wide), jnp.float32),
            pltpu.VMEM((16, cols), jnp.float32),
            pltpu.VMEM((DEPTH, cols), jnp.float32),
            pltpu.VMEM((DEPTH, cols), jnp.bfloat16),
            pltpu.VMEM((cols + DISP, DEPTH), jnp.bfloat16),
            pltpu.VMEM((views - 1, DEPTH, cols), jnp.bfloat16),
            pltpu.VMEM((views - 1, cols + DISP, DEPTH), jnp.bfloat16),
            pltpu.VMEM((512, 256), jnp.float32),
            pltpu.VMEM((512, 256), jnp.float32),
            pltpu.VMEM((1, cols), jnp.float32),
            pltpu.VMEM((1, cols), jnp.float32),
        ],
        compiler_params=pltpu.CompilerParams(vmem_limit_bytes=40 * 1024 * 1024),
        name="match",
    )(meta, bands)


def signal(view, row, disp):
    pl.semaphore_signal(
        pltpu.get_barrier_semaphore(),
        inc=1,
        device_id={"view": view, "row": row, "disp": disp},
        device_id_type=pl.DeviceIdType.MESH,
    )


def remote(source, target, send_sem, recv_sem, view, row, disp):
    return pltpu.make_async_remote_copy(
        src_ref=source,
        dst_ref=target,
        send_sem=send_sem,
        recv_sem=recv_sem,
        device_id={"view": view, "row": row, "disp": disp},
        device_id_type=pl.DeviceIdType.MESH,
    )


def gather_kernel(
    image_ref, pack_ref, bands_ref, meta_ref,
    band_send, band_recv, pack_send, pack_recv, low_send, low_recv, high_send, high_recv,
):
    count = image_ref.shape[0]
    views, bands, disps = (lax.axis_size(axis) for axis in ("view", "row", "disp"))
    view, band, disp = (lax.axis_index(axis) for axis in ("view", "row", "disp"))
    wants_low = [row_of(other, 0, count) < RAD for other in range(views)]
    wants_high = [row_of(other, disps - 1, count) + RAD >= count for other in range(views)]
    get_low = (row_of(view, 0, count) < RAD) & (band > 0)
    get_high = (row_of(view, disps - 1, count) + RAD >= count) & (band < bands - 1)
    has_next = band < bands - 1
    has_previous = band > 0

    for other in range(views):

        @pl.when(view != other)
        def _():
            signal(other, band, disp)

        @pl.when(get_low)
        def _():
            signal(other, band - 1, disp)

        @pl.when(get_high)
        def _():
            signal(other, band + 1, disp)

    expected = views - 1
    expected = expected + jnp.where(has_next, sum(wants_low), 0)
    expected = expected + jnp.where(has_previous, sum(wants_high), 0)
    pl.semaphore_wait(pltpu.get_barrier_semaphore(), expected)

    def band_copy(slot, place, other):
        return remote(
            image_ref, bands_ref.at[place, pl.ds(count, count)],
            band_send.at[slot], band_recv.at[place], other, band, disp,
        )

    def pack_copy(slot, place, other):
        return remote(
            pack_ref, meta_ref.at[place],
            pack_send.at[slot], pack_recv.at[place], other, band, disp,
        )

    def low_copy(slot, place, other):
        return remote(
            image_ref.at[pl.ds(count - RAD, RAD)], bands_ref.at[place, pl.ds(count - RAD, RAD)],
            low_send.at[slot], low_recv.at[place], other, band + 1, disp,
        )

    def high_copy(slot, place, other):
        return remote(
            image_ref.at[pl.ds(0, RAD)], bands_ref.at[place, pl.ds(2 * count, RAD)],
            high_send.at[slot], high_recv.at[place], other, band - 1, disp,
        )

    def sending(step):
        for other in range(views):

            @pl.when(view != other)
            def _():
                step(band_copy(other, view, other))
                step(pack_copy(other, view, other))

            if wants_low[other]:

                @pl.when(has_next)
                def _():
                    step(low_copy(other, view, other))

            if wants_high[other]:

                @pl.when(has_previous)
                def _():
                    step(high_copy(other, view, other))

    sending(lambda copy: copy.start())
    bands_ref[view, pl.ds(count, count), :] = image_ref[...]
    meta_ref[view] = pack_ref[...]

    @pl.when(band == 0)
    def _():
        bands_ref[:, 0:count, :] = jnp.zeros((views, count, image_ref.shape[1]), jnp.float32)

    @pl.when(band == bands - 1)
    def _():
        bands_ref[:, 2 * count : 3 * count, :] = jnp.zeros((views, count, image_ref.shape[1]), jnp.float32)

    for other in range(views):

        @pl.when(view != other)
        def _():
            band_copy(other, other, other).wait_recv()
            pack_copy(other, other, other).wait_recv()

        @pl.when(get_low)
        def _():
            low_copy(other, other, other).wait_recv()

        @pl.when(get_high)
        def _():
            high_copy(other, other, other).wait_recv()

    sending(lambda copy: copy.wait_send())


def gather(image, pack):
    views = lax.axis_size("view")
    rows, cols = image.shape
    vmem = pl.BlockSpec(memory_space=pltpu.VMEM)
    return pl.pallas_call(
        gather_kernel,
        out_shape=(
            jax.ShapeDtypeStruct((views, 3 * rows, cols), jnp.float32),
            jax.ShapeDtypeStruct((views,) + pack.shape, jnp.float32),
        ),
        in_specs=[vmem, vmem],
        out_specs=(vmem, vmem),
        scratch_shapes=[pltpu.SemaphoreType.DMA((views,))] * 8,
        compiler_params=pltpu.CompilerParams(collective_id=0, has_side_effects=True),
        name="gather",
    )(image, pack)


def scatter_kernel(row_count, found_ref, left_ref, right_ref, held_ref, send_sem, recv_sem):
    views, disps = (lax.axis_size(axis) for axis in ("view", "disp"))
    view, band, disp = (lax.axis_index(axis) for axis in ("view", "row", "disp"))
    group = views * disps
    share = group // row_count
    member = view * disps + disp
    mine = row_of(view, disp, row_count)
    sends = member % share == 0
    slots = left_ref.shape[0]
    for row in range(row_count):
        source = row * share

        @pl.when(member != source)
        def _():
            signal(source // disps, band, source % disps)

    @pl.when(sends)
    def _():
        pl.semaphore_wait(pltpu.get_barrier_semaphore(), group - 1)

    def copy(slot, row, place):
        return remote(
            found_ref.at[place // disps], held_ref.at[row],
            send_sem.at[slot], recv_sem.at[row], place // disps, band, place % disps,
        )

    def sending(step):
        for other in range(group):

            @pl.when(sends & (member != other))
            def _():
                step(copy(other, mine, other))

    sending(lambda item: item.start())

    @pl.when(sends)
    def _():
        held_ref[mine] = found_ref[view]

    for row in range(row_count):

        @pl.when(member != row * share)
        def _():
            copy(row, row, row * share).wait_recv()

    for slot in range(slots):
        left_ref[slot] = held_ref[:, slot, :]
        right_ref[slot] = held_ref[:, slots + slot, :]
    sending(lambda item: item.wait_send())


def scatter(found, row_count):
    views, rows, cols = found.shape
    vmem = pl.BlockSpec(memory_space=pltpu.VMEM)
    out = jax.ShapeDtypeStruct((rows // 2, row_count, cols), jnp.float32)
    group = views * lax.axis_size("disp")
    return pl.pallas_call(
        functools.partial(scatter_kernel, row_count),
        out_shape=(out, out),
        in_specs=[vmem],
        out_specs=(vmem, vmem),
        scratch_shapes=[
            pltpu.VMEM((row_count, rows, cols), jnp.float32),
            pltpu.SemaphoreType.DMA((group,)),
            pltpu.SemaphoreType.DMA((row_count,)),
        ],
        compiler_params=pltpu.CompilerParams(collective_id=1, has_side_effects=True),
        name="scatter",
    )(found)


def shards(images, sharpness, paired, offset, row_range):
    image = images[0]
    slots = paired.shape[1]
    ints = jnp.concatenate([paired[0], offset[0], row_range[0].reshape(-1)])
    packed = jnp.concatenate([sharpness, ints.astype(jnp.float32)])
    packed = jnp.pad(packed[None], ((0, 7), (0, 128 - packed.shape[0])))
    bands, meta = gather(image, packed)
    found = match(meta, bands, slots)
    left, right = scatter(found, image.shape[0])
    return (left[None], right[None])


def solution(mesh):
    return jax.shard_map(
        shards,
        mesh=mesh,
        in_specs=(
            P("view", "row", None),
            P("view"),
            P("view", None),
            P("view", None),
            P("view", None, None),
        ),
        out_specs=(P("view", None, "row", None), P("view", None, "row", None)),
        check_vma=False,
    )
```

profile of v0, /device:TPU:13, one launch (start us, length us, event | category | flops | bytes accessed | tf_op | source)
XLA Modules:
  0.0 48.5 jit_solution(15398440937539452224)
XLA Ops:
  1.3 0.0 copy-start.6
  1.3 0.7 %copy-done.6 = s32[1,2,2]{2,1,0:T(2,128)S(1)} copy-done((s32[1,2,2]{2,1,0:T(2,128)S(1)}, s32[1,2,2]{2,1,0:T(2,128)}, u32[]{:S(2)}) %copy-start.6) | copy-done | bytes 40
  2.0 0.0 copy-start.4
  2.0 0.0 copy-start.5
  2.0 0.1 reshape_squeeze.3
  2.0 0.6 %copy-done.4 = s32[1,2]{1,0:T(1,128)S(1)} copy-done((s32[1,2]{1,0:T(1,128)S(1)}, s32[1,2]{1,0:T(1,128)}, u32[]{:S(2)}) %copy-start.4) | copy-done | bytes 32
  2.6 0.0 copy-done.5
  2.6 0.1 add_convert_fusion
  2.7 0.1 maximum_bitcast_fusion
  2.8 0.6 %pad.4.pack_ref = f32[8,128]{1,0:T(8,128)} pad(f32[1,9]{1,0:T(1,128)S(1)} %maximum_bitcast_fusion, f32[]{:T(128)} %constant.2.clone.1), padding=0_7x0_119 | pad | bytes 4136 | tf_op jit(solution)/shard_map/jit(_pad)/pad | solution.py:459
  3.4 9.3 %gather.1 = (f32[4,24,2048]{2,1,0:T(8,128)}, f32[4,8,128]{2,1,0:T(8,128)}) custom-call(f32[8,2048]{1,0:T(8,128)} %bitcast.9, f32[8,128]{1,0:T(8,128)} %pad.4.pack_ref), custom_call_target="tpu_custom_call" | custom-call | tf_op jit(solution)/shard_map/gather/pallas_call | solution.py:369
  12.6 0.0 copy-start
  12.7 1.1 %copy-done = f32[4,24,2048]{2,1,0:T(8,128)S(1)} copy-done((f32[4,24,2048]{2,1,0:T(8,128)S(1)}, f32[4,24,2048]{2,1,0:T(8,128)}, u32[]{:S(2)}) %copy-start) | copy-done | bytes 786456
  13.8 0.0 copy-start.2
  13.8 0.7 %copy-done.2 = f32[4,8,128]{2,1,0:T(8,128)S(1)} copy-done((f32[4,8,128]{2,1,0:T(8,128)S(1)}, f32[4,8,128]{2,1,0:T(8,128)}, u32[]{:S(2)}) %copy-start.2) | copy-done | bytes 16408
  14.5 21.7 %match.1.found_ref = f32[4,4,2048]{2,1,0:T(4,128)S(1)} custom-call(f32[4,8,128]{2,1,0:T(8,128)S(1)} %copy-done.2, f32[4,24,2048]{2,1,0:T(8,128)S(1)} %copy-done), custom_call_target="tpu_custom_call" | custom-call | tf_op jit(solution)/shard_map/match/pallas_call | solution.py:213
  36.2 0.0 copy-start.1
  36.2 0.6 %copy-done.1 = f32[4,4,2048]{2,1,0:T(4,128)} copy-done((f32[4,4,2048]{2,1,0:T(4,128)}, f32[4,4,2048]{2,1,0:T(4,128)S(1)}, u32[]{:S(2)}) %copy-start.1) | copy-done | bytes 131096
  36.8 9.4 %scatter.1 = (f32[2,8,2048]{2,1,0:T(8,128)}, f32[2,8,2048]{2,1,0:T(8,128)}) custom-call(f32[4,4,2048]{2,1,0:T(4,128)} %copy-done.1), custom_call_target="tpu_custom_call" | custom-call | tf_op jit(solution)/shard_map/scatter/pallas_call | solution.py:439
  46.2 0.0 copy-start.3
  46.2 1.6 %copy.10 = f32[1,2,8,2048]{3,2,1,0:T(8,128)} copy(f32[1,2,8,2048]{3,2,1,0:T(8,128)} %bitcast.8) | data formatting | bytes 262144
  47.8 0.0 copy-done.3
  47.8 0.7 %copy.11 = f32[1,2,8,2048]{3,2,1,0:T(8,128)} copy(f32[1,2,8,2048]{3,2,1,0:T(8,128)S(1)} %bitcast.7) | data formatting | bytes 262144
Async XLA Ops:
  1.3 0.7 %copy-start.6 = (s32[1,2,2]{2,1,0:T(2,128)S(1)}, s32[1,2,2]{2,1,0:T(2,128)}, u32[]{:S(2)}) copy-start(s32[1,2,2]{2,1,0:T(2,128)} %param.9) | copy-start | bytes 52
  2.0 0.7 %copy-start.4 = (s32[1,2]{1,0:T(1,128)S(1)}, s32[1,2]{1,0:T(1,128)}, u32[]{:S(2)}) copy-start(s32[1,2]{1,0:T(1,128)} %param.8) | copy-start | bytes 28
  2.0 0.7 %copy-start.5 = (s32[1,2]{1,0:T(1,128)S(1)}, s32[1,2]{1,0:T(1,128)}, u32[]{:S(2)}) copy-start(s32[1,2]{1,0:T(1,128)} %param.7) | copy-start | bytes 28
  12.6 1.1 %copy-start = (f32[4,24,2048]{2,1,0:T(8,128)S(1)}, f32[4,24,2048]{2,1,0:T(8,128)}, u32[]{:S(2)}) copy-start(f32[4,24,2048]{2,1,0:T(8,128)} %get-tuple-element.7.bands_ref) | copy-start | bytes 2359300
  13.8 0.7 %copy-start.2 = (f32[4,8,128]{2,1,0:T(8,128)S(1)}, f32[4,8,128]{2,1,0:T(8,128)}, u32[]{:S(2)}) copy-start(f32[4,8,128]{2,1,0:T(8,128)} %get-tuple-element.6.meta_ref) | copy-start | bytes 49156
  36.2 0.7 %copy-start.1 = (f32[4,4,2048]{2,1,0:T(4,128)}, f32[4,4,2048]{2,1,0:T(4,128)S(1)}, u32[]{:S(2)}) copy-start(f32[4,4,2048]{2,1,0:T(4,128)S(1)} %match.1.found_ref) | copy-start | bytes 393220
  46.2 1.6 %copy-start.3 = (f32[2,8,2048]{2,1,0:T(8,128)S(1)}, f32[2,8,2048]{2,1,0:T(8,128)}, u32[]{:S(2)}) copy-start(f32[2,8,2048]{2,1,0:T(8,128)} %get-tuple-element.9) | copy-start | bytes 393220
where the time goes:
time: 48.8 us; the launch traced here: 48.5 us
  Pallas kernels  40.3 us (83%)
  local copies, waits for them, and re-layouts  6.7 us (14%)
  between operations  1.34 us (3%)
    pallas_call x1, Pallas kernels, match(): pl.pallas_call(functools.partial(match_kernel, views, slots, rows // 3),...  21.7 us
    pallas_call x1, Pallas kernels, scatter(): pl.pallas_call(functools.partial(scatter_kernel, row_count), out_shape=(o...  9.36 us
    pallas_call x1, Pallas kernels, gather(): pl.pallas_call(gather_kernel, out_shape=(jax.ShapeDtypeStruct((views, 3 *...  9.26 us
    unnamed x16, local copies, waits for them, and re-layouts  6.02 us

commit v1 on v0

v1 whole, which is shorter than its diff:
```python
import functools
import math

import jax
import jax.numpy as jnp
from jax import lax
from jax.experimental import pallas as pl
from jax.experimental.pallas import tpu as pltpu
from jax.sharding import PartitionSpec as P

DISP = 256
RAD = 4
TAPS = 2 * RAD + 1
EPSILON = 1e-05
DEPTH = 256
PAD = 128
WIDTH = 512
BLOCK = 256
GRAIN = 16
MARGIN = 384
SPAN = 2 * BLOCK + GRAIN
HALF = 3 * 128 + GRAIN
EXTRA = DEPTH - GRAIN


def rounded(value):
    return value.astype(jnp.bfloat16).astype(jnp.float32)


def split3(value):
    high = rounded(value)
    middle = rounded(value - high)
    return (high, middle, value - high - middle)


def row_of(view, disp, row_count):
    group = lax.axis_size("view") * lax.axis_size("disp")
    return (view * lax.axis_size("disp") + disp) * row_count // group


def segments(row, row_count):
    found = []
    for delta in (-1, 0, 1):
        low = max(row - RAD, delta * row_count)
        high = min(row + RAD + 1, (delta + 1) * row_count)
        for begin, end in ((low, min(high, row + RAD)), (max(low, row + RAD), high)):
            if end > begin:
                found.append((delta, begin - delta * row_count, end - begin, begin - row + RAD))
    return found


def build(window_ref, left_cols, left_rows, right_cols, right_rows, gain):
    cols = left_cols.shape[1]
    sub = lax.broadcasted_iota(jnp.int32, (GRAIN, 128), 0)
    lane = lax.broadcasted_iota(jnp.int32, (GRAIN, DEPTH), 1) - EXTRA
    floor = [-part for part in split3(jnp.full((GRAIN, 128), gain, jnp.float32))]
    zero = jnp.zeros((GRAIN, 128), jnp.float32)
    left_mark, right_mark = (zero, zero)
    for place in range(3):
        left_mark = jnp.where(sub == 3 + place, floor[place], left_mark)
        right_mark = jnp.where(sub == 6 + place, 1.0, right_mark)
    floor = [-part for part in split3(jnp.full((GRAIN, DEPTH), gain, jnp.float32))]
    edge = jnp.zeros((GRAIN, DEPTH), jnp.float32)
    for place in range(6):
        edge = jnp.where(lane == 3 + place, floor[place % 3], edge)
    flag = jnp.where((lane >= 3) & (lane < 9), 1.0, 0.0).astype(jnp.bfloat16)
    left_rows[cols : cols + MARGIN, :] = jnp.concatenate([edge.astype(jnp.bfloat16)] * (MARGIN // GRAIN), axis=0)
    right_rows[0:MARGIN, :] = jnp.concatenate([flag] * (MARGIN // GRAIN), axis=0)
    wide = WIDTH // 128
    left_mark = jnp.concatenate([left_mark] * wide, axis=1)
    right_mark = jnp.concatenate([right_mark] * wide, axis=1)
    place = lax.broadcasted_iota(jnp.int32, (GRAIN, WIDTH), 0)

    def emit(values, end, order, mark, cols_ref, rows_ref, base, row_base):
        for index, value in enumerate(values):
            high = value.astype(jnp.bfloat16)
            parts = (high, (value - high.astype(jnp.float32)).astype(jnp.bfloat16))
            for group in range(3):
                start = (group * len(values) + index) * GRAIN
                cols_ref[start : start + GRAIN, pl.ds(base, WIDTH)] = parts[order[group]]
        high = rounded(end)
        parts = (high, end - high)
        rest = mark
        for group in range(3):
            rest = jnp.where(place == group, parts[order[group]], rest)
        cols_ref[EXTRA:DEPTH, pl.ds(base, WIDTH)] = rest.astype(jnp.bfloat16)
        rows_ref[pl.ds(row_base, WIDTH), :] = cols_ref[:, pl.ds(base, WIDTH)].T

    def body(step, carry):
        base = pl.multiple_of(step * WIDTH, WIDTH)
        main = window_ref[0:8, pl.ds(base, WIDTH + 2 * PAD)]
        last = window_ref[8:9, pl.ds(base, WIDTH + 2 * PAD)]
        taps = [main[:, PAD - RAD + tap : PAD - RAD + tap + WIDTH] for tap in range(TAPS)]
        fan = pltpu.roll(jnp.broadcast_to(last, (8, WIDTH + 2 * PAD)), 0, 1, stride=1, stride_axis=0)
        taps.append(fan[:, PAD - RAD + 7 : PAD - RAD + 7 + WIDTH])
        end = last[:, PAD + RAD : PAD + RAD + WIDTH]
        values = [jnp.concatenate(taps[index : index + 2], axis=0) for index in range(0, TAPS + 1, 2)]
        total = values[0]
        for value in values[1:]:
            total = total + value
        mean = (jnp.sum(total, axis=0, keepdims=True) + end) * (1.0 / (TAPS * TAPS))
        values = [value - mean for value in values]
        end = end - mean
        total = values[0] * values[0]
        for value in values[1:]:
            total = total + value * value
        var = (jnp.sum(total, axis=0, keepdims=True) + end * end) * (1.0 / (TAPS * TAPS))
        scale = lax.rsqrt(var + EPSILON) * (1.0 / TAPS)
        row_base = pl.multiple_of(MARGIN + base, 128)
        emit([value * scale for value in values], end * scale, (0, 0, 1), right_mark, right_cols, right_rows, base, row_base)
        scale = scale * gain
        emit([value * scale for value in values], end * scale, (0, 1, 0), left_mark, left_cols, left_rows, base, base)
        return carry

    lax.fori_loop(0, cols // WIDTH, body, 0)


def soft_half(score_ref, result_ref, column, skip, keep, left):
    lane = lax.broadcasted_iota(jnp.int32, (8, 128), 1)
    sub = lax.broadcasted_iota(jnp.int32, (8, 128), 0)
    skew = lane - sub
    sub_f = sub.astype(jnp.float32)
    lane_f = lane[0:1].astype(jnp.float32)
    slack = 0 if left else 1
    steps = DISP // 8
    corner = 128 // 8

    def load(step):
        return score_ref[pl.ds(8 * step + skip, 8), :]

    near = [skew < 8 * step + slack for step in range(corner)]
    scores = [jnp.where(near[step], load(step), load(step + steps)) for step in range(corner)]
    scores += [load(step) for step in range(corner, steps)]
    tops = scores[:4]
    for step in range(4, steps):
        tops[step % 4] = jnp.maximum(tops[step % 4], scores[step])
    top = jnp.maximum(jnp.maximum(tops[0], tops[1]), jnp.maximum(tops[2], tops[3]))
    top = jnp.broadcast_to(jnp.max(top, axis=0, keepdims=True), (8, 128))
    zero = jnp.zeros((8, 128), jnp.float32)
    summed, running, far = ([zero, zero], [zero, zero], [zero, zero])
    for step in range(steps):
        weight = jnp.exp2(scores[step] - top)
        if step < corner:
            far[step % 2] = far[step % 2] + jnp.where(near[step], 0.0, weight)
        summed[step % 2] = summed[step % 2] + weight
        running[step % 2] = running[step % 2] + summed[step % 2]
    both = summed[0] + summed[1]
    moment = 8.0 * (steps * both - 2.0 * (running[0] + running[1]) + summed[1])
    moment = moment + sub_f * both + float(DISP) * (far[0] + far[1])
    total = jnp.sum(both, axis=0, keepdims=True)
    moment = jnp.sum(moment, axis=0, keepdims=True)
    if left:
        weighted = (lane_f + DISP) * total - moment
    else:
        weighted = moment - lane_f * total
    result_ref[:, pl.ds(column, 128)] = weighted * keep / (total * DISP)


def soft_pair(left_cols, left_rows, right_cols, right_rows, left_score, right_score, left_result, right_result, coarse, fine, keep):
    cols = left_cols.shape[1]
    count = cols // BLOCK

    def scores(rows_ref, row_start, cols_ref, block, score_ref):
        score = jnp.dot(
            rows_ref[pl.ds(row_start * GRAIN, SPAN), :],
            cols_ref[:, pl.ds(pl.multiple_of(block * BLOCK, BLOCK), BLOCK)],
            preferred_element_type=jnp.float32,
        )
        score_ref[0] = score[0:HALF, 0:128]
        score_ref[1] = score[128 : 128 + HALF, 128:256]

    def left_scores(block):
        scores(right_rows, block * (BLOCK // GRAIN) + (MARGIN - BLOCK - GRAIN) // GRAIN - coarse, left_cols, block, left_score)

    def right_scores(block):
        scores(left_rows, block * (BLOCK // GRAIN) + coarse, right_cols, block, right_score)

    def soft(score_ref, result_ref, block, skip, left):
        for half in range(2):
            column = pl.multiple_of(block * BLOCK + half * 128, 128)
            soft_half(score_ref.at[half], result_ref, column, skip, keep, left)

    def body(block, carry):
        right_scores(block)
        soft(left_score, left_result, block, GRAIN - fine, True)
        left_scores(jnp.minimum(block + 1, count - 1))
        soft(right_score, right_result, block, fine, False)
        return carry

    left_scores(0)
    lax.fori_loop(0, count, body, 0, unroll=2)


def place_of(view, row, disp):
    return dict(device_id={"view": view, "row": row, "disp": disp}, device_id_type=pl.DeviceIdType.MESH)


def signal(view, row, disp):
    pl.semaphore_signal(pltpu.get_barrier_semaphore(), inc=1, **place_of(view, row, disp))


def match_kernel(
    slots, image_ref, sharp_ref, paired_ref, offset_ref, range_ref, left_ref, right_ref,
    window, ints, floats, int_table, float_table,
    left_cols, left_rows, right_cols, right_rows, left_score, right_score, result,
    window_send, window_recv, meta_send, meta_recv, table_sem, result_send, result_recv,
):
    count, cols = image_ref.shape
    views, bands, disps = (lax.axis_size(axis) for axis in ("view", "row", "disp"))
    view, band, disp = (lax.axis_index(axis) for axis in ("view", "row", "disp"))
    group = views * disps
    share = group // count
    member = view * disps + disp
    mine = row_of(view, disp, count)
    sends = member % share == 0
    rows_of = [sorted({row_of(other, place, count) for place in range(disps)}) for other in range(views)]

    window[...] = jnp.zeros_like(window)
    left_ref[...] = jnp.zeros_like(left_ref)
    right_ref[...] = jnp.zeros_like(right_ref)
    for slot in range(slots):

        def fill(kind, value):
            ints[view, kind * slots + slot : kind * slots + slot + 1] = value

        shift = jnp.full((1, 128), offset_ref[0, slot], jnp.int32)
        fill(0, jnp.full((1, 128), paired_ref[0, slot], jnp.int32))
        fill(1, shift >> GRAIN.bit_length() - 1)
        fill(2, shift & (GRAIN - 1))
        for end in range(2):
            fill(3 + end, jnp.full((1, 128), range_ref[0, slot, end], jnp.int32))
    floats[view] = jnp.full((8, 128), sharp_ref[0], jnp.float32)

    def inside(row):
        return (row >= 0) & (row < bands)

    for other in range(views):
        for place in range(disps):

            @pl.when((view != other) | (disp != place))
            def _():
                signal(other, band, place)

    expected = group - 1
    for delta in (-1, 1):
        needs = False
        wanted = 0
        for row in range(count):
            has = any(part[0] == delta for part in segments(row, count))
            needs = needs | ((mine == row) & has)
        for other in range(views):
            for row in rows_of[other]:
                if any(part[0] == delta for part in segments(row, count)):
                    wanted = wanted + jnp.where(row_of(other, disp, count) == row, 1, 0)

        @pl.when(needs & inside(band + delta))
        def _():
            for other in range(views):
                signal(other, band + delta, disp)

        expected = expected + jnp.where(inside(band - delta), wanted, 0)
    pl.semaphore_wait(pltpu.get_barrier_semaphore(), expected)

    def window_copy(source, part, index, other, target_band):
        delta, begin, length, place = part
        return pltpu.make_async_remote_copy(
            src_ref=image_ref.at[pl.ds(begin, length)],
            dst_ref=window.at[source, pl.ds(place, length), pl.ds(PAD, cols)],
            send_sem=window_send.at[other, index],
            recv_sem=window_recv.at[source, index],
            **place_of(other, target_band, disp),
        )

    def own_copy(part, index):
        delta, begin, length, place = part
        return pltpu.make_async_copy(
            image_ref.at[pl.ds(begin, length)],
            window.at[view, pl.ds(place, length), pl.ds(PAD, cols)],
            window_recv.at[view, index],
        )

    def meta_copies(source, other):
        return [
            pltpu.make_async_remote_copy(
                src_ref=ref.at[source], dst_ref=ref.at[source],
                send_sem=meta_send.at[other, index], recv_sem=meta_recv.at[source, index],
                **place_of(other, band, disp),
            )
            for index, ref in enumerate((ints, floats))
        ]

    def sending(step, local):
        for other in range(views):

            @pl.when(view != other)
            def _():
                for copy in meta_copies(view, other):
                    step(copy)

            for row in rows_of[other]:
                aimed = row_of(other, disp, count) == row
                for index, part in enumerate(segments(row, count)):
                    if part[0] == 0:

                        @pl.when(aimed & (view != other))
                        def _():
                            step(window_copy(view, part, index, other, band))

                        if local:

                            @pl.when(aimed & (view == other))
                            def _():
                                own_copy(part, index).start()

                    else:

                        @pl.when(aimed & inside(band - part[0]))
                        def _():
                            step(window_copy(view, part, index, other, band - part[0]))

    sending(lambda copy: copy.start(), True)

    for other in range(views):

        @pl.when(view != other)
        def _():
            for copy in meta_copies(other, other):
                copy.wait_recv()

    tables = [
        pltpu.make_async_copy(ints, int_table, table_sem.at[0]),
        pltpu.make_async_copy(floats, float_table, table_sem.at[1]),
    ]
    for copy in tables:
        copy.start()
    for copy in tables:
        copy.wait()

    def arrive(source):
        for row in range(count):
            for index, part in enumerate(segments(row, count)):
                if part[0] == 0:

                    @pl.when((mine == row) & (view != source))
                    def _():
                        window_copy(source, part, index, source, band).wait_recv()

                    @pl.when((mine == row) & (view == source))
                    def _():
                        own_copy(part, index).wait()

                else:

                    @pl.when((mine == row) & inside(band + part[0]))
                    def _():
                        window_copy(source, part, index, source, band + part[0]).wait_recv()

    for source in range(views):
        arrive(source)

    def build_view(source, carry):
        build(
            window.at[source], left_cols.at[source], left_rows.at[source], right_cols.at[source], right_rows.at[source],
            float_table[source, 0, 0] * math.log2(math.e),
        )
        return carry

    lax.fori_loop(0, views, build_view, 0)

    pairs = [(first, slot) for first in range(views - 1) for slot in range(min(slots, views - 1 - first))]

    def outcome(index, first, slot, side, place):
        target = first + side * (slot + 1)
        out = (left_ref, right_ref)[side].at[slot, pl.ds(mine, 1)]
        source = result.at[index, side]
        away = lambda: pltpu.make_async_remote_copy(
            src_ref=source, dst_ref=out,
            send_sem=result_send.at[index, side, place], recv_sem=result_recv.at[mine, side, slot],
            **place_of(target, band, place),
        )
        home = lambda: pltpu.make_async_copy(source, out, result_recv.at[mine, side, slot])
        return target, (away, home)

    def spread(index, first, slot, start):
        for side in range(2):
            for place in range(disps):
                target, (away, home) = outcome(index, first, slot, side, place)
                own = (target == view) & (disp == place)

                @pl.when(sends & jnp.logical_not(own))
                def _():
                    if start:
                        away().start()
                    else:
                        away().wait_send()

                if start:

                    @pl.when(sends & own)
                    def _():
                        home().start()

    def find(index):
        first = sum(jnp.where(index == at, pair[0], 0) for at, pair in enumerate(pairs))
        slot = sum(jnp.where(index == at, pair[1], 0) for at, pair in enumerate(pairs))
        return first, slot

    line = band * count + mine

    def match_pair(index, carry):
        first, slot = find(index)
        partner = first + slot + 1
        begin, end, pairing = (ints[first, pl.ds(kind * slots + slot, 1), :] for kind in (3, 4, 0))
        keep = jnp.where((begin <= line) & (end > line), pairing, 0).astype(jnp.float32)
        soft_pair(
            left_cols.at[first], left_rows.at[first], right_cols.at[partner], right_rows.at[partner],
            left_score, right_score, result.at[index, 0], result.at[index, 1],
            int_table[first, slots + slot, 0], int_table[first, 2 * slots + slot, 0], keep,
        )
        spread(index, first, slot, True)
        return carry

    lax.fori_loop(0, len(pairs), match_pair, 0)

    for row in range(count):
        own = member == row * share
        for side in range(2):
            for slot in range(slots):
                other = view + slot + 1 if side == 0 else view - slot - 1
                exists = (other >= 0) & (other < views)
                out = (left_ref, right_ref)[side].at[slot, pl.ds(row, 1)]
                source = result.at[0, side]

                @pl.when(exists & jnp.logical_not(own))
                def _():
                    pltpu.make_async_remote_copy(
                        src_ref=source, dst_ref=out,
                        send_sem=result_send.at[0, side, 0], recv_sem=result_recv.at[row, side, slot],
                        **place_of(row * share // disps, band, row * share % disps),
                    ).wait_recv()

                @pl.when(exists & own)
                def _():
                    pltpu.make_async_copy(source, out, result_recv.at[row, side, slot]).wait()

    sending(lambda copy: copy.wait_send(), False)
    for index, (first, slot) in enumerate(pairs):
        spread(index, first, slot, False)


def match(image, sharpness, paired, offset, row_range):
    views, disps = (lax.axis_size(axis) for axis in ("view", "disp"))
    count, cols = image.shape
    slots = paired.shape[1]
    pairs = sum(min(slots, views - 1 - first) for first in range(views - 1))
    entries = -(-5 * slots // 8) * 8
    smem = pl.BlockSpec(memory_space=pltpu.SMEM)
    vmem = pl.BlockSpec(memory_space=pltpu.VMEM)
    out = jax.ShapeDtypeStruct((slots, count, cols), jnp.float32)
    dma = pltpu.SemaphoreType.DMA
    return pl.pallas_call(
        functools.partial(match_kernel, slots),
        out_shape=(out, out),
        in_specs=[vmem, smem, smem, smem, smem],
        out_specs=(vmem, vmem),
        scratch_shapes=[
            pltpu.VMEM((views, 16, cols + 2 * PAD), jnp.float32),
            pltpu.VMEM((views, entries, 128), jnp.int32),
            pltpu.VMEM((views, 8, 128), jnp.float32),
            pltpu.SMEM((views, entries, 128), jnp.int32),
            pltpu.SMEM((views, 8, 128), jnp.float32),
            pltpu.VMEM((views, DEPTH, cols), jnp.bfloat16),
            pltpu.VMEM((views, cols + MARGIN, DEPTH), jnp.bfloat16),
            pltpu.VMEM((views, DEPTH, cols), jnp.bfloat16),
            pltpu.VMEM((views, cols + MARGIN, DEPTH), jnp.bfloat16),
            pltpu.VMEM((2, HALF, 128), jnp.float32),
            pltpu.VMEM((2, HALF, 128), jnp.float32),
            pltpu.VMEM((pairs, 2, 1, cols), jnp.float32),
            dma((views, 3)),
            dma((views, 3)),
            dma((views, 2)),
            dma((views, 2)),
            dma((2,)),
            dma((pairs, 2, disps)),
            dma((count, 2, slots)),
        ],
        compiler_params=pltpu.CompilerParams(
            collective_id=0, has_side_effects=True, vmem_limit_bytes=40 * 1024 * 1024
        ),
        name="match",
    )(image, sharpness, paired, offset, row_range)


def shards(images, sharpness, paired, offset, row_range):
    left, right = match(images[0], sharpness, paired, offset, row_range)
    return (left[None], right[None])


def solution(mesh):
    return jax.shard_map(
        shards,
        mesh=mesh,
        in_specs=(
            P("view", "row", None),
            P("view"),
            P("view", None),
            P("view", None),
            P("view", None, None),
        ),
        out_specs=(P("view", None, "row", None), P("view", None, "row", None)),
        check_vma=False,
    )
```

time: 48.8 us -> 45 us (0.922)
  local copies, waits for them, and re-layouts: 6.7 us -> 2.81 us
    unnamed x16 -> x10, local copies, waits for them, and re-layouts: 6.02 us -> 2.81 us
    pad x1 -> x0, local copies, waits for them, and re-layouts: 0.6 us -> none  [shards(): packed = jnp.pad(packed[None], ((0, 7), (0, 128 - packed.shape[0])))]
    pallas_call x3 -> x1, Pallas kernels: 40.3 us -> 40.7 us  [match(): pl.pallas_call(functools.partial(match_kernel, slots), out_shape=(out, ou...]
where the time goes in v1:
time: 45 us; the launch traced here: 44.8 us
  Pallas kernels  40.7 us (90%)
  local copies, waits for them, and re-layouts  2.81 us (6%)
  between operations  1.33 us (3%)
    pallas_call x1, Pallas kernels, match(): pl.pallas_call(functools.partial(match_kernel, slots), out_shape=(out, ou...  40.7 us
    unnamed x10, local copies, waits for them, and re-layouts  2.81 us

profile of v1, /device:TPU:13, one launch (start us, length us, event | category | flops | bytes accessed | tf_op | source)
XLA Modules:
  0.0 44.8 jit_solution(2701537496131919592)
XLA Ops:
  0.6 0.0 copy-start.3
  1.3 0.0 copy-start.1
  1.3 0.0 copy-start.2
  1.3 0.0 copy-done.3
  1.3 0.7 %copy-done.1 = s32[1,2,2]{2,1,0:T(2,128)S(1)} copy-done((s32[1,2,2]{2,1,0:T(2,128)S(1)}, s32[1,2,2]{2,1,0:T(2,128)}, u32[]{:S(2)}) %copy-start.1) | copy-done | bytes 40
  2.0 0.0 copy-done.2
  2.0 0.0 copy-start
  2.0 0.8 %copy-done = f32[1,8,2048]{2,1,0:T(8,128)S(1)} copy-done((f32[1,8,2048]{2,1,0:T(8,128)S(1)}, f32[1,8,2048]{2,1,0:T(8,128)}, u32[]{:S(2)}) %copy-start) | copy-done | bytes 65560
  2.8 40.7 %match.1 = (f32[2,8,2048]{2,1,0:T(8,128)S(1)}, f32[2,8,2048]{2,1,0:T(8,128)S(1)}) custom-call(f32[8,2048]{1,0:T(8,128)S(1)} %bitcast.5, f32[1]{0:T(128)S(6)} %copy.9.sharp_ref, s32[1,2]{1,0:T(1,128)S(1)} %copy-done.2, s32[1,2]{1,0:T(1,128)S(1)} %copy-done.3, s32[1,2,2]{2,1,0:T(2,128)S(1)} %copy-done.1), custom_call_target="tpu_custom_call" | custom-call | tf_op jit(solution)/shard_map/match/pallas_call | solution.py:461
  43.5 0.7 %copy.10 = f32[1,2,8,2048]{3,2,1,0:T(8,128)} copy(f32[1,2,8,2048]{3,2,1,0:T(8,128)S(1)} %bitcast.4) | data formatting | bytes 262144
  44.1 0.7 %copy.11 = f32[1,2,8,2048]{3,2,1,0:T(8,128)} copy(f32[1,2,8,2048]{3,2,1,0:T(8,128)S(1)} %bitcast.3) | data formatting | bytes 262144
Async XLA Ops:
  0.6 0.7 %copy-start.3 = (s32[1,2]{1,0:T(1,128)S(1)}, s32[1,2]{1,0:T(1,128)}, u32[]{:S(2)}) copy-start(s32[1,2]{1,0:T(1,128)} %offset_ref.1) | copy-start | bytes 28
  1.3 0.7 %copy-start.1 = (s32[1,2,2]{2,1,0:T(2,128)S(1)}, s32[1,2,2]{2,1,0:T(2,128)}, u32[]{:S(2)}) copy-start(s32[1,2,2]{2,1,0:T(2,128)} %range_ref.1) | copy-start | bytes 52
  1.3 0.7 %copy-start.2 = (s32[1,2]{1,0:T(1,128)S(1)}, s32[1,2]{1,0:T(1,128)}, u32[]{:S(2)}) copy-start(s32[1,2]{1,0:T(1,128)} %paired_ref.1) | copy-start | bytes 28
  2.0 0.8 %copy-start = (f32[1,8,2048]{2,1,0:T(8,128)S(1)}, f32[1,8,2048]{2,1,0:T(8,128)}, u32[]{:S(2)}) copy-start(f32[1,8,2048]{2,1,0:T(8,128)} %param.5) | copy-start | bytes 196612

commit v2 on v1

--- a/solution.py
+++ b/solution.py
@@ -14,7 +14,6 @@
 EPSILON = 1e-05
 DEPTH = 256
 PAD = 128
-WIDTH = 512
 BLOCK = 256
 GRAIN = 16
 MARGIN = 384
@@ -49,70 +48,69 @@
     return found
 
 
-def build(window_ref, left_cols, left_rows, right_cols, right_rows, gain):
-    cols = left_cols.shape[1]
+def tiled(row, width):
+    return jnp.concatenate([row] * (width // 128), axis=1)
+
+
+def emit(values, end, order, mark, cols_ref):
+    for index, value in enumerate(values):
+        high = value.astype(jnp.bfloat16)
+        parts = (high, (value - high.astype(jnp.float32)).astype(jnp.bfloat16))
+        for group in range(3):
+            start = (group * len(values) + index) * GRAIN
+            cols_ref[start : start + GRAIN, :] = parts[order[group]]
+    high = rounded(end)
+    parts = (high, end - high)
+    place = lax.broadcasted_iota(jnp.int32, (GRAIN, end.shape[1]), 0)
+    rest = mark
+    for group in range(3):
+        rest = jnp.where(place == group, parts[order[group]], rest)
+    cols_ref[EXTRA:DEPTH, :] = rest.astype(jnp.bfloat16)
+
+
+def build(window_ref, gain, left_refs, right_refs):
+    cols = window_ref.shape[1] - 2 * PAD
     sub = lax.broadcasted_iota(jnp.int32, (GRAIN, 128), 0)
     lane = lax.broadcasted_iota(jnp.int32, (GRAIN, DEPTH), 1) - EXTRA
-    floor = [-part for part in split3(jnp.full((GRAIN, 128), gain, jnp.float32))]
+    main = window_ref[0:8, :]
+    last = window_ref[8:9, :]
+    taps = [main[:, PAD - RAD + tap : PAD - RAD + tap + cols] for tap in range(TAPS)]
+    fan = pltpu.roll(jnp.broadcast_to(last, main.shape), 0, 1, stride=1, stride_axis=0)
+    taps.append(fan[:, PAD - RAD + 7 : PAD - RAD + 7 + cols])
+    end = last[:, PAD + RAD : PAD + RAD + cols]
+    values = [jnp.concatenate(taps[index : index + 2], axis=0) for index in range(0, TAPS + 1, 2)]
+    total = values[0]
+    for value in values[1:]:
+        total = total + value
+    mean = (jnp.sum(total, axis=0, keepdims=True) + end) * (1.0 / (TAPS * TAPS))
+    values = [value - mean for value in values]
+    end = end - mean
+    total = values[0] * values[0]
+    for value in values[1:]:
+        total = total + value * value
+    var = (jnp.sum(total, axis=0, keepdims=True) + end * end) * (1.0 / (TAPS * TAPS))
+    scale = lax.rsqrt(var + EPSILON) * (1.0 / TAPS)
     zero = jnp.zeros((GRAIN, 128), jnp.float32)
-    left_mark, right_mark = (zero, zero)
-    for place in range(3):
-        left_mark = jnp.where(sub == 3 + place, floor[place], left_mark)
-        right_mark = jnp.where(sub == 6 + place, 1.0, right_mark)
-    floor = [-part for part in split3(jnp.full((GRAIN, DEPTH), gain, jnp.float32))]
-    edge = jnp.zeros((GRAIN, DEPTH), jnp.float32)
-    for place in range(6):
-        edge = jnp.where(lane == 3 + place, floor[place % 3], edge)
-    flag = jnp.where((lane >= 3) & (lane < 9), 1.0, 0.0).astype(jnp.bfloat16)
-    left_rows[cols : cols + MARGIN, :] = jnp.concatenate([edge.astype(jnp.bfloat16)] * (MARGIN // GRAIN), axis=0)
-    right_rows[0:MARGIN, :] = jnp.concatenate([flag] * (MARGIN // GRAIN), axis=0)
-    wide = WIDTH // 128
-    left_mark = jnp.concatenate([left_mark] * wide, axis=1)
-    right_mark = jnp.concatenate([right_mark] * wide, axis=1)
-    place = lax.broadcasted_iota(jnp.int32, (GRAIN, WIDTH), 0)
-
-    def emit(values, end, order, mark, cols_ref, rows_ref, base, row_base):
-        for index, value in enumerate(values):
-            high = value.astype(jnp.bfloat16)
-            parts = (high, (value - high.astype(jnp.float32)).astype(jnp.bfloat16))
-            for group in range(3):
-                start = (group * len(values) + index) * GRAIN
-                cols_ref[start : start + GRAIN, pl.ds(base, WIDTH)] = parts[order[group]]
-        high = rounded(end)
-        parts = (high, end - high)
-        rest = mark
-        for group in range(3):
-            rest = jnp.where(place == group, parts[order[group]], rest)
-        cols_ref[EXTRA:DEPTH, pl.ds(base, WIDTH)] = rest.astype(jnp.bfloat16)
-        rows_ref[pl.ds(row_base, WIDTH), :] = cols_ref[:, pl.ds(base, WIDTH)].T
-
-    def body(step, carry):
-        base = pl.multiple_of(step * WIDTH, WIDTH)
-        main = window_ref[0:8, pl.ds(base, WIDTH + 2 * PAD)]
-        last = window_ref[8:9, pl.ds(base, WIDTH + 2 * PAD)]
-        taps = [main[:, PAD - RAD + tap : PAD - RAD + tap + WIDTH] for tap in range(TAPS)]
-        fan = pltpu.roll(jnp.broadcast_to(last, (8, WIDTH + 2 * PAD)), 0, 1, stride=1, stride_axis=0)
-        taps.append(fan[:, PAD - RAD + 7 : PAD - RAD + 7 + WIDTH])
-        end = last[:, PAD + RAD : PAD + RAD + WIDTH]
-        values = [jnp.concatenate(taps[index : index + 2], axis=0) for index in range(0, TAPS + 1, 2)]
-        total = values[0]
-        for value in values[1:]:
-            total = total + value
-        mean = (jnp.sum(total, axis=0, keepdims=True) + end) * (1.0 / (TAPS * TAPS))
-        values = [value - mean for value in values]
-        end = end - mean
-        total = values[0] * values[0]
-        for value in values[1:]:
-            total = total + value * value
-        var = (jnp.sum(total, axis=0, keepdims=True) + end * end) * (1.0 / (TAPS * TAPS))
-        scale = lax.rsqrt(var + EPSILON) * (1.0 / TAPS)
-        row_base = pl.multiple_of(MARGIN + base, 128)
-        emit([value * scale for value in values], end * scale, (0, 0, 1), right_mark, right_cols, right_rows, base, row_base)
-        scale = scale * gain
-        emit([value * scale for value in values], end * scale, (0, 1, 0), left_mark, left_cols, left_rows, base, base)
-        return carry
-
-    lax.fori_loop(0, cols // WIDTH, body, 0)
+    if right_refs is not None:
+        cols_ref, rows_ref = right_refs
+        mark = jnp.where((sub >= 6) & (sub < 9), 1.0, zero)
+        emit([value * scale for value in values], end * scale, (0, 0, 1), tiled(mark, cols), cols_ref)
+        rows_ref[MARGIN : MARGIN + cols, :] = cols_ref[...].T
+        flag = jnp.where((lane >= 3) & (lane < 9), 1.0, 0.0).astype(jnp.bfloat16)
+        rows_ref[0:MARGIN, :] = jnp.concatenate([flag] * (MARGIN // GRAIN), axis=0)
+    if left_refs is not None:
+        cols_ref, rows_ref = left_refs
+        floor = [-part for part in split3(jnp.broadcast_to(gain, (GRAIN, 128)))]
+        mark = zero
+        for place in range(3):
+            mark = jnp.where(sub == 3 + place, floor[place], mark)
+        scale = scale * tiled(gain, cols)
+        emit([value * scale for value in values], end * scale, (0, 1, 0), tiled(mark, cols), cols_ref)
+        rows_ref[0:cols, :] = cols_ref[...].T
+        edge = jnp.zeros((GRAIN, DEPTH), jnp.float32)
+        for place in range(6):
+            edge = jnp.where(lane == 3 + place, tiled(floor[place % 3], DEPTH), edge)
+        rows_ref[cols : cols + MARGIN, :] = jnp.concatenate([edge.astype(jnp.bfloat16)] * (MARGIN // GRAIN), axis=0)
 
 
 def soft_half(score_ref, result_ref, column, skip, keep, left):
@@ -188,7 +186,7 @@
         return carry
 
     left_scores(0)
-    lax.fori_loop(0, count, body, 0, unroll=2)
+    lax.fori_loop(0, count, body, 0, unroll=True)
 
 
 def place_of(view, row, disp):
@@ -200,10 +198,10 @@
 
 
 def match_kernel(
-    slots, image_ref, sharp_ref, paired_ref, offset_ref, range_ref, left_ref, right_ref,
-    window, ints, floats, int_table, float_table,
+    slots, image_ref, sharp_hbm, paired_hbm, offset_hbm, range_hbm, left_ref, right_ref,
+    sharp_ref, paired_ref, offset_ref, range_ref, window, ints, floats, int_table,
     left_cols, left_rows, right_cols, right_rows, left_score, right_score, result,
-    window_send, window_recv, meta_send, meta_recv, table_sem, result_send, result_recv,
+    window_send, window_recv, meta_send, meta_recv, scalar_sem, table_sem, result_send, result_recv,
 ):
     count, cols = image_ref.shape
     views, bands, disps = (lax.axis_size(axis) for axis in ("view", "row", "disp"))
@@ -215,21 +213,17 @@
     sends = member % share == 0
     rows_of = [sorted({row_of(other, place, count) for place in range(disps)}) for other in range(views)]
 
+    scalars = [
+        pltpu.make_async_copy(source, target, scalar_sem.at[index])
+        for index, (source, target) in enumerate(
+            ((sharp_hbm, sharp_ref), (paired_hbm, paired_ref), (offset_hbm, offset_ref), (range_hbm, range_ref))
+        )
+    ]
+    for copy in scalars:
+        copy.start()
     window[...] = jnp.zeros_like(window)
     left_ref[...] = jnp.zeros_like(left_ref)
     right_ref[...] = jnp.zeros_like(right_ref)
-    for slot in range(slots):
-
-        def fill(kind, value):
-            ints[view, kind * slots + slot : kind * slots + slot + 1] = value
-
-        shift = jnp.full((1, 128), offset_ref[0, slot], jnp.int32)
-        fill(0, jnp.full((1, 128), paired_ref[0, slot], jnp.int32))
-        fill(1, shift >> GRAIN.bit_length() - 1)
-        fill(2, shift & (GRAIN - 1))
-        for end in range(2):
-            fill(3 + end, jnp.full((1, 128), range_ref[0, slot, end], jnp.int32))
-    floats[view] = jnp.full((8, 128), sharp_ref[0], jnp.float32)
 
     def inside(row):
         return (row >= 0) & (row < bands)
@@ -259,6 +253,20 @@
                 signal(other, band + delta, disp)
 
         expected = expected + jnp.where(inside(band - delta), wanted, 0)
+    for copy in scalars:
+        copy.wait()
+    for slot in range(slots):
+
+        def fill(kind, value):
+            ints[view, kind * slots + slot : kind * slots + slot + 1] = value
+
+        shift = jnp.broadcast_to(offset_ref[0:1, slot : slot + 1], (1, 128))
+        fill(0, jnp.broadcast_to(paired_ref[0:1, slot : slot + 1], (1, 128)))
+        fill(1, shift >> GRAIN.bit_length() - 1)
+        fill(2, shift & (GRAIN - 1))
+        for end in range(2):
+            fill(3 + end, jnp.broadcast_to(range_ref[0, slot : slot + 1, end : end + 1], (1, 128)))
+    floats[view] = jnp.broadcast_to(sharp_ref[...], (8, 128))
     pl.semaphore_wait(pltpu.get_barrier_semaphore(), expected)
 
     def window_copy(source, part, index, other, target_band):
@@ -327,14 +335,8 @@
             for copy in meta_copies(other, other):
                 copy.wait_recv()
 
-    tables = [
-        pltpu.make_async_copy(ints, int_table, table_sem.at[0]),
-        pltpu.make_async_copy(floats, float_table, table_sem.at[1]),
-    ]
-    for copy in tables:
-        copy.start()
-    for copy in tables:
-        copy.wait()
+    table = pltpu.make_async_copy(ints, int_table, table_sem)
+    table.start()
 
     def arrive(source):
         for row in range(count):
@@ -357,15 +359,12 @@
 
     for source in range(views):
         arrive(source)
-
-    def build_view(source, carry):
         build(
-            window.at[source], left_cols.at[source], left_rows.at[source], right_cols.at[source], right_rows.at[source],
-            float_table[source, 0, 0] * math.log2(math.e),
-        )
-        return carry
-
-    lax.fori_loop(0, views, build_view, 0)
+            window.at[source], floats[source, 0:1, :] * math.log2(math.e),
+            (left_cols.at[source], left_rows.at[source]) if source < views - 1 else None,
+            (right_cols.at[source - 1], right_rows.at[source - 1]) if source > 0 else None,
+        )
+    table.wait()
 
     pairs = [(first, slot) for first in range(views - 1) for slot in range(min(slots, views - 1 - first))]
 
@@ -413,7 +412,7 @@
         begin, end, pairing = (ints[first, pl.ds(kind * slots + slot, 1), :] for kind in (3, 4, 0))
         keep = jnp.where((begin <= line) & (end > line), pairing, 0).astype(jnp.float32)
         soft_pair(
-            left_cols.at[first], left_rows.at[first], right_cols.at[partner], right_rows.at[partner],
+            left_cols.at[first], left_rows.at[first], right_cols.at[partner - 1], right_rows.at[partner - 1],
             left_score, right_score, result.at[index, 0], result.at[index, 1],
             int_table[first, slots + slot, 0], int_table[first, 2 * slots + slot, 0], keep,
         )
@@ -454,25 +453,28 @@
     slots = paired.shape[1]
     pairs = sum(min(slots, views - 1 - first) for first in range(views - 1))
     entries = -(-5 * slots // 8) * 8
-    smem = pl.BlockSpec(memory_space=pltpu.SMEM)
+    hbm = pl.BlockSpec(memory_space=pl.ANY)
     vmem = pl.BlockSpec(memory_space=pltpu.VMEM)
     out = jax.ShapeDtypeStruct((slots, count, cols), jnp.float32)
     dma = pltpu.SemaphoreType.DMA
     return pl.pallas_call(
         functools.partial(match_kernel, slots),
         out_shape=(out, out),
-        in_specs=[vmem, smem, smem, smem, smem],
+        in_specs=[hbm] * 5,
         out_specs=(vmem, vmem),
         scratch_shapes=[
+            pltpu.VMEM(sharpness.shape, jnp.float32),
+            pltpu.VMEM(paired.shape, jnp.int32),
+            pltpu.VMEM(offset.shape, jnp.int32),
+            pltpu.VMEM(row_range.shape, jnp.int32),
             pltpu.VMEM((views, 16, cols + 2 * PAD), jnp.float32),
             pltpu.VMEM((views, entries, 128), jnp.int32),
             pltpu.VMEM((views, 8, 128), jnp.float32),
             pltpu.SMEM((views, entries, 128), jnp.int32),
-            pltpu.SMEM((views, 8, 128), jnp.float32),
-            pltpu.VMEM((views, DEPTH, cols), jnp.bfloat16),
-            pltpu.VMEM((views, cols + MARGIN, DEPTH), jnp.bfloat16),
-            pltpu.VMEM((views, DEPTH, cols), jnp.bfloat16),
-            pltpu.VMEM((views, cols + MARGIN, DEPTH), jnp.bfloat16),
+            pltpu.VMEM((views - 1, DEPTH, cols), jnp.bfloat16),
+            pltpu.VMEM((views - 1, cols + MARGIN, DEPTH), jnp.bfloat16),
+            pltpu.VMEM((views - 1, DEPTH, cols), jnp.bfloat16),
+            pltpu.VMEM((views - 1, cols + MARGIN, DEPTH), jnp.bfloat16),
             pltpu.VMEM((2, HALF, 128), jnp.float32),
             pltpu.VMEM((2, HALF, 128), jnp.float32),
             pltpu.VMEM((pairs, 2, 1, cols), jnp.float32),
@@ -480,7 +482,8 @@
             dma((views, 3)),
             dma((views, 2)),
             dma((views, 2)),
-            dma((2,)),
+            dma((4,)),
+            dma,
             dma((pairs, 2, disps)),
             dma((count, 2, slots)),
         ],
@@ -492,7 +495,7 @@
 
 
 def shards(images, sharpness, paired, offset, row_range):
-    left, right = match(images[0], sharpness, paired, offset, row_range)
+    left, right = match(images[0], sharpness[None], paired, offset, row_range)
     return (left[None], right[None])
 
 

time: 45 us -> 34.6 us (0.77)
  Pallas kernels: 40.7 us -> 30.3 us
    pallas_call x1, Pallas kernels: 40.7 us -> 30.3 us  [match(): pl.pallas_call(functools.partial(match_kernel, slots), out_shape=(out, ou...]
where the time goes in v2:
time: 34.6 us; the launch traced here: 34.4 us
  Pallas kernels  30.3 us (88%)
  local copies, waits for them, and re-layouts  2.83 us (8%)
  between operations  1.31 us (4%)
    pallas_call x1, Pallas kernels, match(): pl.pallas_call(functools.partial(match_kernel, slots), out_shape=(out, ou...  30.3 us
    unnamed x10, local copies, waits for them, and re-layouts  2.83 us

profile of v2, /device:TPU:13, one launch (start us, length us, event | category | flops | bytes accessed | tf_op | source)
XLA Modules:
  0.0 34.4 jit_solution(2224533868947724884)
XLA Ops:
  1.3 0.0 copy-start.3
  1.3 0.0 copy-start.1
  1.3 0.0 copy-start.2
  1.3 0.6 %copy-done.3 = s32[1,2]{1,0:T(1,128)S(1)} copy-done((s32[1,2]{1,0:T(1,128)S(1)}, s32[1,2]{1,0:T(1,128)}, u32[]{:S(2)}) %copy-start.3) | copy-done | bytes 32
  1.9 0.0 copy-done.1
  2.0 0.0 copy-done.2
  2.0 0.0 copy-start
  2.0 0.8 %copy-done = f32[1,8,2048]{2,1,0:T(8,128)S(1)} copy-done((f32[1,8,2048]{2,1,0:T(8,128)S(1)}, f32[1,8,2048]{2,1,0:T(8,128)}, u32[]{:S(2)}) %copy-start) | copy-done | bytes 65560
  2.8 30.3 %match.1 = (f32[2,8,2048]{2,1,0:T(8,128)S(1)}, f32[2,8,2048]{2,1,0:T(8,128)S(1)}) custom-call(f32[8,2048]{1,0:T(8,128)S(1)} %bitcast.7, f32[1,1]{1,0:T(1,128)} %bitcast.4.sharp_hbm, s32[1,2]{1,0:T(1,128)S(1)} %copy-done.2, s32[1,2]{1,0:T(1,128)S(1)} %copy-done.3, s32[1,2,2]{2,1,0:T(2,128)S(1)} %copy-done.1), custom_call_target="tpu_custom_call" | custom-call | tf_op jit(solution)/shard_map/match/pallas_call | solution.py:460
  33.1 0.7 %copy.10 = f32[1,2,8,2048]{3,2,1,0:T(8,128)} copy(f32[1,2,8,2048]{3,2,1,0:T(8,128)S(1)} %bitcast.6) | data formatting | bytes 262144
  33.8 0.7 %copy.11 = f32[1,2,8,2048]{3,2,1,0:T(8,128)} copy(f32[1,2,8,2048]{3,2,1,0:T(8,128)S(1)} %bitcast.5) | data formatting | bytes 262144
Async XLA Ops:
  1.3 0.7 %copy-start.3 = (s32[1,2]{1,0:T(1,128)S(1)}, s32[1,2]{1,0:T(1,128)}, u32[]{:S(2)}) copy-start(s32[1,2]{1,0:T(1,128)} %offset_hbm.1) | copy-start | bytes 28
  1.3 0.7 %copy-start.1 = (s32[1,2,2]{2,1,0:T(2,128)S(1)}, s32[1,2,2]{2,1,0:T(2,128)}, u32[]{:S(2)}) copy-start(s32[1,2,2]{2,1,0:T(2,128)} %range_hbm.1) | copy-start | bytes 52
  1.3 0.7 %copy-start.2 = (s32[1,2]{1,0:T(1,128)S(1)}, s32[1,2]{1,0:T(1,128)}, u32[]{:S(2)}) copy-start(s32[1,2]{1,0:T(1,128)} %paired_hbm.1) | copy-start | bytes 28
  2.0 0.8 %copy-start = (f32[1,8,2048]{2,1,0:T(8,128)S(1)}, f32[1,8,2048]{2,1,0:T(8,128)}, u32[]{:S(2)}) copy-start(f32[1,8,2048]{2,1,0:T(8,128)} %param.5) | copy-start | bytes 196612

commit v3 on v2

--- a/solution.py
+++ b/solution.py
@@ -17,8 +17,8 @@
 BLOCK = 256
 GRAIN = 16
 MARGIN = 384
-SPAN = 2 * BLOCK + GRAIN
-HALF = 3 * 128 + GRAIN
+SPAN = 2 * BLOCK
+HALF = 3 * 128
 EXTRA = DEPTH - GRAIN
 
 
@@ -113,7 +113,41 @@
         rows_ref[cols : cols + MARGIN, :] = jnp.concatenate([edge.astype(jnp.bfloat16)] * (MARGIN // GRAIN), axis=0)
 
 
-def soft_half(score_ref, result_ref, column, skip, keep, left):
+def turned(tiles, amount, forward):
+    lane = lax.broadcasted_iota(jnp.int32, tiles[0].shape, 1)
+    count = len(tiles)
+    if forward:
+        moved = [pltpu.roll(tile, amount, 1) for tile in tiles]
+        return [jnp.where(lane < amount, moved[index - 1], moved[index]) for index in range(count)]
+    moved = [pltpu.roll(tile, (128 - amount) & 127, 1) for tile in tiles]
+    return [jnp.where(lane < 128 - amount, moved[index], moved[(index + 1) % count]) for index in range(count)]
+
+
+class Turn:
+    def __init__(self, source_ref, target_ref, amount, forward):
+        self.source, self.target, self.forward = source_ref, target_ref, forward
+        self.amount = amount if forward else (128 - amount) & 127
+        self.edge = amount if forward else 128 - amount
+        self.moved = {}
+
+    def tile(self, index):
+        if index not in self.moved:
+            self.moved[index] = pltpu.roll(self.source[:, index * 128 : index * 128 + 128], self.amount, 1)
+        return self.moved[index]
+
+    def block(self, block):
+        count = self.source.shape[1] // 128
+        wide = BLOCK // 128
+        for index in range(block * wide, block * wide + wide):
+            lane = lax.broadcasted_iota(jnp.int32, (DEPTH, 128), 1)
+            if self.forward:
+                tile = jnp.where(lane < self.edge, self.tile(max(index - 1, 0)), self.tile(index))
+            else:
+                tile = jnp.where(lane < self.edge, self.tile(index), self.tile(min(index + 1, count - 1)))
+            self.target[:, index * 128 : index * 128 + 128] = tile
+
+
+def soft_half(score_ref, result_ref, column, left):
     lane = lax.broadcasted_iota(jnp.int32, (8, 128), 1)
     sub = lax.broadcasted_iota(jnp.int32, (8, 128), 0)
     skew = lane - sub
@@ -124,7 +158,7 @@
     corner = 128 // 8
 
     def load(step):
-        return score_ref[pl.ds(8 * step + skip, 8), :]
+        return score_ref[8 * step : 8 * step + 8, :]
 
     near = [skew < 8 * step + slack for step in range(corner)]
     scores = [jnp.where(near[step], load(step), load(step + steps)) for step in range(corner)]
@@ -151,42 +185,61 @@
         weighted = (lane_f + DISP) * total - moment
     else:
         weighted = moment - lane_f * total
-    result_ref[:, pl.ds(column, 128)] = weighted * keep / (total * DISP)
-
-
-def soft_pair(left_cols, left_rows, right_cols, right_rows, left_score, right_score, left_result, right_result, coarse, fine, keep):
+    result_ref[:, column : column + 128] = weighted / (total * DISP)
+
+
+def soft_pair(
+    left_cols, left_rows, right_cols, right_rows, left_turned, right_turned, left_score, right_score, raw,
+    left_result, right_result, coarse, fine, keep,
+):
     cols = left_cols.shape[1]
     count = cols // BLOCK
+    left_turn = Turn(left_cols, left_turned, fine, False)
+    right_turn = Turn(right_cols, right_turned, fine, True)
 
     def scores(rows_ref, row_start, cols_ref, block, score_ref):
         score = jnp.dot(
             rows_ref[pl.ds(row_start * GRAIN, SPAN), :],
-            cols_ref[:, pl.ds(pl.multiple_of(block * BLOCK, BLOCK), BLOCK)],
+            cols_ref[:, block * BLOCK : (block + 1) * BLOCK],
             preferred_element_type=jnp.float32,
         )
         score_ref[0] = score[0:HALF, 0:128]
         score_ref[1] = score[128 : 128 + HALF, 128:256]
 
     def left_scores(block):
-        scores(right_rows, block * (BLOCK // GRAIN) + (MARGIN - BLOCK - GRAIN) // GRAIN - coarse, left_cols, block, left_score)
+        scores(right_rows, block * (BLOCK // GRAIN) + (MARGIN - BLOCK) // GRAIN - coarse, left_turned, block, left_score)
 
     def right_scores(block):
-        scores(left_rows, block * (BLOCK // GRAIN) + coarse, right_cols, block, right_score)
-
-    def soft(score_ref, result_ref, block, skip, left):
+        scores(left_rows, block * (BLOCK // GRAIN) + coarse, right_turned, block, right_score)
+
+    def soft(score_ref, side, block, left):
         for half in range(2):
-            column = pl.multiple_of(block * BLOCK + half * 128, 128)
-            soft_half(score_ref.at[half], result_ref, column, skip, keep, left)
-
-    def body(block, carry):
+            soft_half(score_ref.at[half], raw.at[side], block * BLOCK + half * 128, left)
+
+    left_turn.block(0)
+    left_scores(0)
+    right_turn.block(0)
+    for block in range(count):
         right_scores(block)
-        soft(left_score, left_result, block, GRAIN - fine, True)
-        left_scores(jnp.minimum(block + 1, count - 1))
-        soft(right_score, right_result, block, fine, False)
-        return carry
-
-    left_scores(0)
-    lax.fori_loop(0, count, body, 0, unroll=True)
+        if block + 1 < count:
+            left_turn.block(block + 1)
+        soft(left_score, 0, block, True)
+        if block + 1 < count:
+            left_scores(block + 1)
+            right_turn.block(block + 1)
+        soft(right_score, 1, block, False)
+
+    even = (DISP - 1) / (2.0 * DISP)
+    lane = lax.broadcasted_iota(jnp.int32, (1, 128), 1)
+    for side, result_ref in enumerate((left_result, right_result)):
+        tiles = [jnp.broadcast_to(raw[side, :, start : start + 128], (8, 128)) for start in range(0, cols, 128)]
+        tiles = [tile[0:1] for tile in turned(tiles, fine, side == 0)]
+        if side == 0:
+            tiles[0] = jnp.where(lane < fine, even, tiles[0])
+        else:
+            tiles[-1] = jnp.where(lane >= 128 - fine, even, tiles[-1])
+        for index, tile in enumerate(tiles):
+            result_ref[:, index * 128 : index * 128 + 128] = tile * keep
 
 
 def place_of(view, row, disp):
@@ -200,7 +253,7 @@
 def match_kernel(
     slots, image_ref, sharp_hbm, paired_hbm, offset_hbm, range_hbm, left_ref, right_ref,
     sharp_ref, paired_ref, offset_ref, range_ref, window, ints, floats, int_table,
-    left_cols, left_rows, right_cols, right_rows, left_score, right_score, result,
+    left_cols, left_rows, right_cols, right_rows, left_turned, right_turned, left_score, right_score, raw, result,
     window_send, window_recv, meta_send, meta_recv, scalar_sem, table_sem, result_send, result_recv,
 ):
     count, cols = image_ref.shape
@@ -279,12 +332,12 @@
             **place_of(other, target_band, disp),
         )
 
-    def own_copy(part, index):
+    def own_copy(source, part, index):
         delta, begin, length, place = part
         return pltpu.make_async_copy(
             image_ref.at[pl.ds(begin, length)],
-            window.at[view, pl.ds(place, length), pl.ds(PAD, cols)],
-            window_recv.at[view, index],
+            window.at[source, pl.ds(place, length), pl.ds(PAD, cols)],
+            window_recv.at[source, index],
         )
 
     def meta_copies(source, other):
@@ -306,25 +359,29 @@
                     step(copy)
 
             for row in rows_of[other]:
-                aimed = row_of(other, disp, count) == row
-                for index, part in enumerate(segments(row, count)):
-                    if part[0] == 0:
-
-                        @pl.when(aimed & (view != other))
+
+                @pl.when(row_of(other, disp, count) == row)
+                def _():
+                    for index, part in enumerate(segments(row, count)):
+                        if part[0] != 0:
+
+                            @pl.when(inside(band - part[0]))
+                            def _():
+                                step(window_copy(view, part, index, other, band - part[0]))
+
+                    @pl.when(view != other)
+                    def _():
+                        for index, part in enumerate(segments(row, count)):
+                            if part[0] == 0:
+                                step(window_copy(view, part, index, other, band))
+
+                    if local:
+
+                        @pl.when(view == other)
                         def _():
-                            step(window_copy(view, part, index, other, band))
-
-                        if local:
-
-                            @pl.when(aimed & (view == other))
-                            def _():
-                                own_copy(part, index).start()
-
-                    else:
-
-                        @pl.when(aimed & inside(band - part[0]))
-                        def _():
-                            step(window_copy(view, part, index, other, band - part[0]))
+                            for index, part in enumerate(segments(row, count)):
+                                if part[0] == 0:
+                                    own_copy(view, part, index).start()
 
     sending(lambda copy: copy.start(), True)
 
@@ -340,22 +397,14 @@
 
     def arrive(source):
         for row in range(count):
-            for index, part in enumerate(segments(row, count)):
-                if part[0] == 0:
-
-                    @pl.when((mine == row) & (view != source))
-                    def _():
-                        window_copy(source, part, index, source, band).wait_recv()
-
-                    @pl.when((mine == row) & (view == source))
-                    def _():
-                        own_copy(part, index).wait()
-
-                else:
-
-                    @pl.when((mine == row) & inside(band + part[0]))
-                    def _():
-                        window_copy(source, part, index, source, band + part[0]).wait_recv()
+
+            @pl.when(mine == row)
+            def _():
+                for index, part in enumerate(segments(row, count)):
+                    if part[0] == 0:
+                        own_copy(source, part, index).wait()
+                    else:
+                        pl.when(inside(band + part[0]))(own_copy(source, part, index).wait)
 
     for source in range(views):
         arrive(source)
@@ -374,10 +423,10 @@
         source = result.at[index, side]
         away = lambda: pltpu.make_async_remote_copy(
             src_ref=source, dst_ref=out,
-            send_sem=result_send.at[index, side, place], recv_sem=result_recv.at[mine, side, slot],
+            send_sem=result_send.at[index, side, place], recv_sem=result_recv.at[side, slot],
             **place_of(target, band, place),
         )
-        home = lambda: pltpu.make_async_copy(source, out, result_recv.at[mine, side, slot])
+        home = lambda: pltpu.make_async_copy(source, out, result_recv.at[side, slot])
         return target, (away, home)
 
     def spread(index, first, slot, start):
@@ -413,38 +462,25 @@
         keep = jnp.where((begin <= line) & (end > line), pairing, 0).astype(jnp.float32)
         soft_pair(
             left_cols.at[first], left_rows.at[first], right_cols.at[partner - 1], right_rows.at[partner - 1],
-            left_score, right_score, result.at[index, 0], result.at[index, 1],
+            left_turned, right_turned, left_score, right_score, raw, result.at[index, 0], result.at[index, 1],
             int_table[first, slots + slot, 0], int_table[first, 2 * slots + slot, 0], keep,
         )
         spread(index, first, slot, True)
         return carry
 
     lax.fori_loop(0, len(pairs), match_pair, 0)
-
-    for row in range(count):
-        own = member == row * share
-        for side in range(2):
-            for slot in range(slots):
-                other = view + slot + 1 if side == 0 else view - slot - 1
-                exists = (other >= 0) & (other < views)
-                out = (left_ref, right_ref)[side].at[slot, pl.ds(row, 1)]
-                source = result.at[0, side]
-
-                @pl.when(exists & jnp.logical_not(own))
-                def _():
-                    pltpu.make_async_remote_copy(
-                        src_ref=source, dst_ref=out,
-                        send_sem=result_send.at[0, side, 0], recv_sem=result_recv.at[row, side, slot],
-                        **place_of(row * share // disps, band, row * share % disps),
-                    ).wait_recv()
-
-                @pl.when(exists & own)
-                def _():
-                    pltpu.make_async_copy(source, out, result_recv.at[row, side, slot]).wait()
 
     sending(lambda copy: copy.wait_send(), False)
     for index, (first, slot) in enumerate(pairs):
         spread(index, first, slot, False)
+    for side in range(2):
+        for slot in range(slots):
+            other = view + slot + 1 if side == 0 else view - slot - 1
+
+            @pl.when((other >= 0) & (other < views))
+            def _():
+                out = (left_ref, right_ref)[side].at[slot]
+                pltpu.make_async_copy(out, out, result_recv.at[side, slot]).wait()
 
 
 def match(image, sharpness, paired, offset, row_range):
@@ -475,8 +511,11 @@
             pltpu.VMEM((views - 1, cols + MARGIN, DEPTH), jnp.bfloat16),
             pltpu.VMEM((views - 1, DEPTH, cols), jnp.bfloat16),
             pltpu.VMEM((views - 1, cols + MARGIN, DEPTH), jnp.bfloat16),
+            pltpu.VMEM((DEPTH, cols), jnp.bfloat16),
+            pltpu.VMEM((DEPTH, cols), jnp.bfloat16),
             pltpu.VMEM((2, HALF, 128), jnp.float32),
             pltpu.VMEM((2, HALF, 128), jnp.float32),
+            pltpu.VMEM((2, 1, cols), jnp.float32),
             pltpu.VMEM((pairs, 2, 1, cols), jnp.float32),
             dma((views, 3)),
             dma((views, 3)),
@@ -485,7 +524,7 @@
             dma((4,)),
             dma,
             dma((pairs, 2, disps)),
-            dma((count, 2, slots)),
+            dma((2, slots)),
         ],
         compiler_params=pltpu.CompilerParams(
             collective_id=0, has_side_effects=True, vmem_limit_bytes=40 * 1024 * 1024
@@ -494,8 +533,33 @@
     )(image, sharpness, paired, offset, row_range)
 
 
+def settle_kernel(left_ref, right_ref, left_out, right_out, sems):
+    copies = [
+        pltpu.make_async_copy(source, target, sems.at[index])
+        for index, (source, target) in enumerate(((left_ref, left_out), (right_ref, right_out)))
+    ]
+    for copy in copies:
+        copy.start()
+    for copy in copies:
+        copy.wait()
+
+
+def settle(left, right):
+    anywhere = pl.BlockSpec(memory_space=pl.ANY)
+    return pl.pallas_call(
+        settle_kernel,
+        out_shape=(left, right),
+        in_specs=[pl.BlockSpec(memory_space=pltpu.VMEM)] * 2,
+        out_specs=(anywhere, anywhere),
+        scratch_shapes=[pltpu.SemaphoreType.DMA((2,))],
+        compiler_params=pltpu.CompilerParams(vmem_limit_bytes=16 * 1024 * 1024),
+        name="settle",
+    )(left, right)
+
+
 def shards(images, sharpness, paired, offset, row_range):
     left, right = match(images[0], sharpness[None], paired, offset, row_range)
+    left, right = settle(left, right)
     return (left[None], right[None])
 
 

time: 34.6 us -> 33 us (0.954)
  local copies, waits for them, and re-layouts: 2.83 us -> 1.51 us
    unnamed x10 -> x8, local copies, waits for them, and re-layouts: 2.83 us -> 1.51 us
    pallas_call x1, Pallas kernels: 30.3 us -> 29.2 us  [match(): pl.pallas_call(functools.partial(match_kernel, slots), out_shape=(out, ou...]
    pallas_call x0 -> x1, Pallas kernels: none -> 0.72 us  [settle(): pl.pallas_call(settle_kernel, out_shape=(left, right), in_specs=[pl.Block...]
where the time goes in v3:
time: 33 us; the launch traced here: 32.8 us
  Pallas kernels  30 us (91%)
  local copies, waits for them, and re-layouts  1.51 us (5%)
  between operations  1.31 us (4%)
    pallas_call x1, Pallas kernels, match(): pl.pallas_call(functools.partial(match_kernel, slots), out_shape=(out, ou...  29.2 us
    unnamed x8, local copies, waits for them, and re-layouts  1.51 us
    pallas_call x1, Pallas kernels, settle(): pl.pallas_call(settle_kernel, out_shape=(left, right), in_specs=[pl.Block...  0.72 us

profile of v3, /device:TPU:13, one launch (start us, length us, event | category | flops | bytes accessed | tf_op | source)
XLA Modules:
  0.0 32.8 jit_solution(11267486769979757399)
XLA Ops:
  1.3 0.0 copy-start.3
  1.3 0.0 copy-start.1
  1.3 0.0 copy-start.2
  1.3 0.6 %copy-done.3 = s32[1,2]{1,0:T(1,128)S(1)} copy-done((s32[1,2]{1,0:T(1,128)S(1)}, s32[1,2]{1,0:T(1,128)}, u32[]{:S(2)}) %copy-start.3) | copy-done | bytes 32
  1.9 0.0 copy-done.1
  2.0 0.0 copy-done.2
  2.0 0.0 copy-start
  2.0 0.8 %copy-done = f32[1,8,2048]{2,1,0:T(8,128)S(1)} copy-done((f32[1,8,2048]{2,1,0:T(8,128)S(1)}, f32[1,8,2048]{2,1,0:T(8,128)}, u32[]{:S(2)}) %copy-start) | copy-done | bytes 65560
  2.8 29.2 %match.1 = (f32[2,8,2048]{2,1,0:T(8,128)S(1)}, f32[2,8,2048]{2,1,0:T(8,128)S(1)}) custom-call(f32[8,2048]{1,0:T(8,128)S(1)} %bitcast.5, f32[1,1]{1,0:T(1,128)} %bitcast.4.sharp_hbm, s32[1,2]{1,0:T(1,128)S(1)} %copy-done.2, s32[1,2]{1,0:T(1,128)S(1)} %copy-done.3, s32[1,2,2]{2,1,0:T(2,128)S(1)} %copy-done.1), custom_call_target="tpu_custom_call" | custom-call | tf_op jit(solution)/shard_map/match/pallas_call | solution.py:496
  32.1 0.7 %settle.1 = (f32[2,8,2048]{2,1,0:T(8,128)}, f32[2,8,2048]{2,1,0:T(8,128)}) custom-call(f32[2,8,2048]{2,1,0:T(8,128)S(1)} %get-tuple-element.6.left_ref, f32[2,8,2048]{2,1,0:T(8,128)S(1)} %get-tuple-element.7.right_ref), custom_call_target="tpu_custom_call" | custom-call | tf_op jit(solution)/shard_map/settle/pallas_call | solution.py:549
Async XLA Ops:
  1.3 0.7 %copy-start.3 = (s32[1,2]{1,0:T(1,128)S(1)}, s32[1,2]{1,0:T(1,128)}, u32[]{:S(2)}) copy-start(s32[1,2]{1,0:T(1,128)} %offset_hbm.1) | copy-start | bytes 28
  1.3 0.7 %copy-start.1 = (s32[1,2,2]{2,1,0:T(2,128)S(1)}, s32[1,2,2]{2,1,0:T(2,128)}, u32[]{:S(2)}) copy-start(s32[1,2,2]{2,1,0:T(2,128)} %range_hbm.1) | copy-start | bytes 52
  1.3 0.7 %copy-start.2 = (s32[1,2]{1,0:T(1,128)S(1)}, s32[1,2]{1,0:T(1,128)}, u32[]{:S(2)}) copy-start(s32[1,2]{1,0:T(1,128)} %paired_hbm.1) | copy-start | bytes 28
  2.0 0.8 %copy-start = (f32[1,8,2048]{2,1,0:T(8,128)S(1)}, f32[1,8,2048]{2,1,0:T(8,128)}, u32[]{:S(2)}) copy-start(f32[1,8,2048]{2,1,0:T(8,128)} %param.5) | copy-start | bytes 196612

commit v4 on v3

--- a/solution.py
+++ b/solution.py
@@ -79,16 +79,20 @@
     taps.append(fan[:, PAD - RAD + 7 : PAD - RAD + 7 + cols])
     end = last[:, PAD + RAD : PAD + RAD + cols]
     values = [jnp.concatenate(taps[index : index + 2], axis=0) for index in range(0, TAPS + 1, 2)]
-    total = values[0]
-    for value in values[1:]:
-        total = total + value
-    mean = (jnp.sum(total, axis=0, keepdims=True) + end) * (1.0 / (TAPS * TAPS))
+    width = main.shape[1]
+    sub8 = lax.broadcasted_iota(jnp.int32, main.shape, 0)
+    sums = jnp.sum(main, axis=0, keepdims=True) + last
+    squares = jnp.sum(main * main, axis=0, keepdims=True) + last * last
+    total = jnp.where(sub8 < 4, sums, squares)
+    double = total + pltpu.roll(total, width - 1, 1)
+    double = double + pltpu.roll(double, width - 2, 1)
+    double = double + pltpu.roll(double, width - 4, 1)
+    total = double + pltpu.roll(total, width - 8, 1)
+    total = total[:, PAD - RAD : PAD - RAD + cols] * (1.0 / (TAPS * TAPS))
+    mean = total[0:1]
+    var = total[4:5] - mean * mean
     values = [value - mean for value in values]
     end = end - mean
-    total = values[0] * values[0]
-    for value in values[1:]:
-        total = total + value * value
-    var = (jnp.sum(total, axis=0, keepdims=True) + end * end) * (1.0 / (TAPS * TAPS))
     scale = lax.rsqrt(var + EPSILON) * (1.0 / TAPS)
     zero = jnp.zeros((GRAIN, 128), jnp.float32)
     if right_refs is not None:
@@ -129,22 +133,32 @@
         self.amount = amount if forward else (128 - amount) & 127
         self.edge = amount if forward else 128 - amount
         self.moved = {}
-
-    def tile(self, index):
-        if index not in self.moved:
-            self.moved[index] = pltpu.roll(self.source[:, index * 128 : index * 128 + 128], self.amount, 1)
-        return self.moved[index]
+        size = EXTRA // 3
+        self.parts = [(0, size), (2 * size, DEPTH)] if forward else [(0, 2 * size), (EXTRA, DEPTH)]
+        self.copy = size if forward else 2 * size
+
+    def tile(self, index, part):
+        if (index, part) not in self.moved:
+            begin, end = part
+            self.moved[index, part] = pltpu.roll(self.source[begin:end, index * 128 : index * 128 + 128], self.amount, 1)
+        return self.moved[index, part]
 
     def block(self, block):
         count = self.source.shape[1] // 128
         wide = BLOCK // 128
+        size = EXTRA // 3
         for index in range(block * wide, block * wide + wide):
-            lane = lax.broadcasted_iota(jnp.int32, (DEPTH, 128), 1)
-            if self.forward:
-                tile = jnp.where(lane < self.edge, self.tile(max(index - 1, 0)), self.tile(index))
-            else:
-                tile = jnp.where(lane < self.edge, self.tile(index), self.tile(min(index + 1, count - 1)))
-            self.target[:, index * 128 : index * 128 + 128] = tile
+            place = slice(index * 128, index * 128 + 128)
+            for part in self.parts:
+                begin, end = part
+                lane = lax.broadcasted_iota(jnp.int32, (end - begin, 128), 1)
+                if self.forward:
+                    tile = jnp.where(lane < self.edge, self.tile(max(index - 1, 0), part), self.tile(index, part))
+                else:
+                    tile = jnp.where(lane < self.edge, self.tile(index, part), self.tile(min(index + 1, count - 1), part))
+                self.target[begin:end, place] = tile
+                if begin == 0:
+                    self.target[self.copy : self.copy + size, place] = tile[0:size]
 
 
 def soft_half(score_ref, result_ref, column, left):

time: 33 us -> 31.7 us (0.961)
  Pallas kernels: 30 us -> 28.7 us
    pallas_call x1, Pallas kernels: 29.2 us -> 28 us  [match(): pl.pallas_call(functools.partial(match_kernel, slots), out_shape=(out, ou...]
where the time goes in v4:
time: 31.7 us; the launch traced here: 31.5 us
  Pallas kernels  28.7 us (91%)
  local copies, waits for them, and re-layouts  1.51 us (5%)
  between operations  1.31 us (4%)
    pallas_call x1, Pallas kernels, match(): pl.pallas_call(functools.partial(match_kernel, slots), out_shape=(out, ou...  28 us
    unnamed x8, local copies, waits for them, and re-layouts  1.51 us
    pallas_call x1, Pallas kernels, settle(): pl.pallas_call(settle_kernel, out_shape=(left, right), in_specs=[pl.Block...  0.72 us

profile of v4, /device:TPU:13, one launch (start us, length us, event | category | flops | bytes accessed | tf_op | source)
XLA Modules:
  0.0 31.5 jit_solution(17304287262355712295)
XLA Ops:
  1.3 0.0 copy-start.3
  1.3 0.0 copy-start.1
  1.3 0.0 copy-start.2
  1.3 0.6 %copy-done.3 = s32[1,2]{1,0:T(1,128)S(1)} copy-done((s32[1,2]{1,0:T(1,128)S(1)}, s32[1,2]{1,0:T(1,128)}, u32[]{:S(2)}) %copy-start.3) | copy-done | bytes 32
  1.9 0.0 copy-done.1
  2.0 0.0 copy-done.2
  2.0 0.0 copy-start
  2.0 0.8 %copy-done = f32[1,8,2048]{2,1,0:T(8,128)S(1)} copy-done((f32[1,8,2048]{2,1,0:T(8,128)S(1)}, f32[1,8,2048]{2,1,0:T(8,128)}, u32[]{:S(2)}) %copy-start) | copy-done | bytes 65560
  2.8 28.0 %match.1 = (f32[2,8,2048]{2,1,0:T(8,128)S(1)}, f32[2,8,2048]{2,1,0:T(8,128)S(1)}) custom-call(f32[8,2048]{1,0:T(8,128)S(1)} %bitcast.5, f32[1,1]{1,0:T(1,128)} %bitcast.4.sharp_hbm, s32[1,2]{1,0:T(1,128)S(1)} %copy-done.2, s32[1,2]{1,0:T(1,128)S(1)} %copy-done.3, s32[1,2,2]{2,1,0:T(2,128)S(1)} %copy-done.1), custom_call_target="tpu_custom_call" | custom-call | tf_op jit(solution)/shard_map/match/pallas_call | solution.py:510
  30.8 0.7 %settle.1 = (f32[2,8,2048]{2,1,0:T(8,128)}, f32[2,8,2048]{2,1,0:T(8,128)}) custom-call(f32[2,8,2048]{2,1,0:T(8,128)S(1)} %get-tuple-element.6.left_ref, f32[2,8,2048]{2,1,0:T(8,128)S(1)} %get-tuple-element.7.right_ref), custom_call_target="tpu_custom_call" | custom-call | tf_op jit(solution)/shard_map/settle/pallas_call | solution.py:563
Async XLA Ops:
  1.3 0.7 %copy-start.3 = (s32[1,2]{1,0:T(1,128)S(1)}, s32[1,2]{1,0:T(1,128)}, u32[]{:S(2)}) copy-start(s32[1,2]{1,0:T(1,128)} %offset_hbm.1) | copy-start | bytes 28
  1.3 0.7 %copy-start.1 = (s32[1,2,2]{2,1,0:T(2,128)S(1)}, s32[1,2,2]{2,1,0:T(2,128)}, u32[]{:S(2)}) copy-start(s32[1,2,2]{2,1,0:T(2,128)} %range_hbm.1) | copy-start | bytes 52
  1.3 0.7 %copy-start.2 = (s32[1,2]{1,0:T(1,128)S(1)}, s32[1,2]{1,0:T(1,128)}, u32[]{:S(2)}) copy-start(s32[1,2]{1,0:T(1,128)} %paired_hbm.1) | copy-start | bytes 28
  2.0 0.8 %copy-start = (f32[1,8,2048]{2,1,0:T(8,128)S(1)}, f32[1,8,2048]{2,1,0:T(8,128)}, u32[]{:S(2)}) copy-start(f32[1,8,2048]{2,1,0:T(8,128)} %param.5) | copy-start | bytes 196612

commit v5 on v4

--- a/solution.py
+++ b/solution.py
@@ -267,7 +267,7 @@
 def match_kernel(
     slots, image_ref, sharp_hbm, paired_hbm, offset_hbm, range_hbm, left_ref, right_ref,
     sharp_ref, paired_ref, offset_ref, range_ref, window, ints, floats, int_table,
-    left_cols, left_rows, right_cols, right_rows, left_turned, right_turned, left_score, right_score, raw, result,
+    left_cols, left_rows, right_cols, right_rows, left_turned, right_turned, left_score, right_score, raw, result, empty,
     window_send, window_recv, meta_send, meta_recv, scalar_sem, table_sem, result_send, result_recv,
 ):
     count, cols = image_ref.shape
@@ -289,8 +289,18 @@
     for copy in scalars:
         copy.start()
     window[...] = jnp.zeros_like(window)
-    left_ref[...] = jnp.zeros_like(left_ref)
-    right_ref[...] = jnp.zeros_like(right_ref)
+    empty[...] = jnp.zeros_like(empty)
+
+    def clearing(step):
+        for side in range(2):
+            for slot in range(slots):
+                other = view + slot + 1 if side == 0 else view - slot - 1
+
+                @pl.when((other < 0) | (other >= views))
+                def _():
+                    step(pltpu.make_async_copy(empty, (left_ref, right_ref)[side].at[slot], result_recv.at[side, slot]))
+
+    clearing(lambda copy: copy.start())
 
     def inside(row):
         return (row >= 0) & (row < bands)
@@ -487,6 +497,7 @@
     sending(lambda copy: copy.wait_send(), False)
     for index, (first, slot) in enumerate(pairs):
         spread(index, first, slot, False)
+    clearing(lambda copy: copy.wait())
     for side in range(2):
         for slot in range(slots):
             other = view + slot + 1 if side == 0 else view - slot - 1
@@ -503,15 +514,14 @@
     slots = paired.shape[1]
     pairs = sum(min(slots, views - 1 - first) for first in range(views - 1))
     entries = -(-5 * slots // 8) * 8
-    hbm = pl.BlockSpec(memory_space=pl.ANY)
-    vmem = pl.BlockSpec(memory_space=pltpu.VMEM)
+    anywhere = pl.BlockSpec(memory_space=pl.ANY)
     out = jax.ShapeDtypeStruct((slots, count, cols), jnp.float32)
     dma = pltpu.SemaphoreType.DMA
     return pl.pallas_call(
         functools.partial(match_kernel, slots),
         out_shape=(out, out),
-        in_specs=[hbm] * 5,
-        out_specs=(vmem, vmem),
+        in_specs=[anywhere] * 5,
+        out_specs=(anywhere, anywhere),
         scratch_shapes=[
             pltpu.VMEM(sharpness.shape, jnp.float32),
             pltpu.VMEM(paired.shape, jnp.int32),
@@ -531,6 +541,7 @@
             pltpu.VMEM((2, HALF, 128), jnp.float32),
             pltpu.VMEM((2, 1, cols), jnp.float32),
             pltpu.VMEM((pairs, 2, 1, cols), jnp.float32),
+            pltpu.VMEM((count, cols), jnp.float32),
             dma((views, 3)),
             dma((views, 3)),
             dma((views, 2)),
@@ -541,21 +552,27 @@
             dma((2, slots)),
         ],
         compiler_params=pltpu.CompilerParams(
-            collective_id=0, has_side_effects=True, vmem_limit_bytes=40 * 1024 * 1024
+            collective_id=0, has_side_effects=True, vmem_limit_bytes=62 * 1000 * 1000
         ),
         name="match",
     )(image, sharpness, paired, offset, row_range)
 
 
-def settle_kernel(left_ref, right_ref, left_out, right_out, sems):
-    copies = [
-        pltpu.make_async_copy(source, target, sems.at[index])
-        for index, (source, target) in enumerate(((left_ref, left_out), (right_ref, right_out)))
-    ]
-    for copy in copies:
-        copy.start()
-    for copy in copies:
-        copy.wait()
+def settle_kernel(left_ref, right_ref, left_out, right_out, held, sems):
+    sides = ((left_ref, left_out), (right_ref, right_out))
+    slots = left_ref.shape[0]
+    inward = [[pltpu.make_async_copy(source.at[slot], held.at[side, slot], sems.at[0, side, slot]) for slot in range(slots)] for side, (source, target) in enumerate(sides)]
+    outward = [[pltpu.make_async_copy(held.at[side, slot], target.at[slot], sems.at[1, side, slot]) for slot in range(slots)] for side, (source, target) in enumerate(sides)]
+    for group in inward:
+        for copy in group:
+            copy.start()
+    for ahead, after in zip(inward, outward):
+        for first, second in zip(ahead, after):
+            first.wait()
+            second.start()
+    for group in outward:
+        for copy in group:
+            copy.wait()
 
 
 def settle(left, right):
@@ -563,10 +580,10 @@
     return pl.pallas_call(
         settle_kernel,
         out_shape=(left, right),
-        in_specs=[pl.BlockSpec(memory_space=pltpu.VMEM)] * 2,
+        in_specs=[anywhere] * 2,
         out_specs=(anywhere, anywhere),
-        scratch_shapes=[pltpu.SemaphoreType.DMA((2,))],
-        compiler_params=pltpu.CompilerParams(vmem_limit_bytes=16 * 1024 * 1024),
+        scratch_shapes=[pltpu.VMEM((2, *left.shape), jnp.float32), pltpu.SemaphoreType.DMA((2, 2, left.shape[0]))],
+        compiler_params=pltpu.CompilerParams(vmem_limit_bytes=62 * 1000 * 1000),
         name="settle",
     )(left, right)
 

time: 31.7 us -> 31.4 us (level)
  local copies, waits for them, and re-layouts: 1.51 us -> 0 us
  Pallas kernels: 28.7 us -> 29.9 us
    unnamed x8 -> x0, local copies, waits for them, and re-layouts: 1.51 us -> none
    pallas_call x1, Pallas kernels: 0.72 us -> 1.63 us  [settle(): pl.pallas_call(settle_kernel, out_shape=(left, right), in_specs=[anywhere...]
where the time goes in v5:
time: 31.4 us; the launch traced here: 31.2 us
  Pallas kernels  29.9 us (95%)
  between operations  1.28 us (4%)
    pallas_call x1, Pallas kernels, match(): pl.pallas_call(functools.partial(match_kernel, slots), out_shape=(out, ou...  28.2 us
    pallas_call x1, Pallas kernels, settle(): pl.pallas_call(settle_kernel, out_shape=(left, right), in_specs=[anywhere...  1.63 us

profile of v5, /device:TPU:13, one launch (start us, length us, event | category | flops | bytes accessed | tf_op | source)
XLA Modules:
  0.0 31.2 jit_solution(10833780611837645997)
XLA Ops:
  1.3 28.2 %match.1 = (f32[2,8,2048]{2,1,0:T(8,128)}, f32[2,8,2048]{2,1,0:T(8,128)}) custom-call(f32[8,2048]{1,0:T(8,128)} %bitcast.5, f32[1,1]{1,0:T(1,128)} %bitcast.4.sharp_hbm, s32[1,2]{1,0:T(1,128)} %paired_hbm.1, s32[1,2]{1,0:T(1,128)} %offset_hbm.1, s32[1,2,2]{2,1,0:T(2,128)} %range_hbm.1), custom_call_target="tpu_custom_call" | custom-call | tf_op jit(solution)/shard_map/match/pallas_call | solution.py:520
  29.5 1.6 %settle.1 = (f32[2,8,2048]{2,1,0:T(8,128)}, f32[2,8,2048]{2,1,0:T(8,128)}) custom-call(f32[2,8,2048]{2,1,0:T(8,128)} %get-tuple-element.6.left_ref, f32[2,8,2048]{2,1,0:T(8,128)} %get-tuple-element.7.right_ref), custom_call_target="tpu_custom_call" | custom-call | tf_op jit(solution)/shard_map/settle/pallas_call | solution.py:580

commit v6 on v5

--- a/solution.py
+++ b/solution.py
@@ -234,13 +234,13 @@
     left_scores(0)
     right_turn.block(0)
     for block in range(count):
-        right_scores(block)
         if block + 1 < count:
             left_turn.block(block + 1)
+            right_turn.block(block + 1)
+        right_scores(block)
         soft(left_score, 0, block, True)
         if block + 1 < count:
             left_scores(block + 1)
-            right_turn.block(block + 1)
         soft(right_score, 1, block, False)
 
     even = (DISP - 1) / (2.0 * DISP)
@@ -288,19 +288,13 @@
     ]
     for copy in scalars:
         copy.start()
-    window[...] = jnp.zeros_like(window)
-    empty[...] = jnp.zeros_like(empty)
-
-    def clearing(step):
-        for side in range(2):
-            for slot in range(slots):
-                other = view + slot + 1 if side == 0 else view - slot - 1
-
-                @pl.when((other < 0) | (other >= views))
-                def _():
-                    step(pltpu.make_async_copy(empty, (left_ref, right_ref)[side].at[slot], result_recv.at[side, slot]))
-
-    clearing(lambda copy: copy.start())
+    for start in (0, PAD + cols):
+        window[:, :, start : start + PAD] = jnp.zeros((views, 16, PAD), jnp.float32)
+
+    @pl.when(((mine < RAD) & (band == 0)) | ((mine + RAD >= count) & (band == bands - 1)))
+    def _():
+        window[...] = jnp.zeros_like(window)
+
 
     def inside(row):
         return (row >= 0) & (row < bands)
@@ -330,6 +324,19 @@
                 signal(other, band + delta, disp)
 
         expected = expected + jnp.where(inside(band - delta), wanted, 0)
+    empty[...] = jnp.zeros_like(empty)
+
+    def clearing(step):
+        for side in range(2):
+            for slot in range(slots):
+                other = view + slot + 1 if side == 0 else view - slot - 1
+
+                @pl.when((other < 0) | (other >= views))
+                def _():
+                    step(pltpu.make_async_copy(empty, (left_ref, right_ref)[side].at[slot], result_recv.at[side, slot]))
+
+    clearing(lambda copy: copy.start())
+
     for copy in scalars:
         copy.wait()
     for slot in range(slots):

time: 31.4 us -> 31.4 us (level)
  no operation moved by 1% of the time
where the time goes in v6:
time: 31.4 us; the launch traced here: 31.2 us
  Pallas kernels  29.9 us (95%)
  between operations  1.28 us (4%)
    pallas_call x1, Pallas kernels, match(): pl.pallas_call(functools.partial(match_kernel, slots), out_shape=(out, ou...  28.3 us
    pallas_call x1, Pallas kernels, settle(): pl.pallas_call(settle_kernel, out_shape=(left, right), in_specs=[anywhere...  1.63 us

profile of v6, /device:TPU:13, one launch (start us, length us, event | category | flops | bytes accessed | tf_op | source)
XLA Modules:
  0.0 31.2 jit_solution(15089394650267873297)
XLA Ops:
  1.3 28.3 %match.1 = (f32[2,8,2048]{2,1,0:T(8,128)}, f32[2,8,2048]{2,1,0:T(8,128)}) custom-call(f32[8,2048]{1,0:T(8,128)} %bitcast.5, f32[1,1]{1,0:T(1,128)} %bitcast.4.sharp_hbm, s32[1,2]{1,0:T(1,128)} %paired_hbm.1, s32[1,2]{1,0:T(1,128)} %offset_hbm.1, s32[1,2,2]{2,1,0:T(2,128)} %range_hbm.1), custom_call_target="tpu_custom_call" | custom-call | tf_op jit(solution)/shard_map/match/pallas_call | solution.py:527
  29.6 1.6 %settle.1 = (f32[2,8,2048]{2,1,0:T(8,128)}, f32[2,8,2048]{2,1,0:T(8,128)}) custom-call(f32[2,8,2048]{2,1,0:T(8,128)} %get-tuple-element.6.left_ref, f32[2,8,2048]{2,1,0:T(8,128)} %get-tuple-element.7.right_ref), custom_call_target="tpu_custom_call" | custom-call | tf_op jit(solution)/shard_map/settle/pallas_call | solution.py:587
